TPU v7x, 32 devices: a whole 2x2x4 slice. The times are simulated.
32 devices in a mesh: group: 2 (over y), ctx: 8 (over z, core), head: 2 (over x).
Axes of the slice: x: 2, y: 2, z: 4, core: 2. Of those that a mesh axis runs over, the one named last changes fastest.
Arguments:
- queries: bfloat16 [2048, 4096], P(('group', 'ctx'), 'head'), parts along dimension 0, may hold values from -6 to 6
- keys: bfloat16 [2048, 512], P(('group', 'ctx'), 'head'), parts along dimension 0, may hold values from -6 to 6
- values: bfloat16 [2048, 512], P(('group', 'ctx'), 'head'), parts along dimension 0, may hold values from -6 to 6
- sinks: float32 [64], P('head'), may hold values from 0 to 4
- segments: int32 [2048], P('group'), parts along dimension 0, may hold values from 0 to 3, never falling along the last dimension, each value on 1 to 768 neighbouring positions
- hidden_in: bfloat16 [2048, 2880], P(('group', 'ctx')), parts along dimension 0, may hold values from -6 to 6
- routes: int32 [2048, 4], P(('group', 'ctx')), parts along dimension 0, may hold values from 0 to 7, all different within a row; in each aligned block of 64 rows (0 to 63, 64 to 127, ...) at most 48 rows name the same one
- w_out: bfloat16 [4096, 2880], P('head'), may hold values from -0.09375 to 0.09375
- norm_gain: float32 [2880], replicated, may hold values from 0.1 to 1.9
- router: bfloat16 [2880, 8], replicated, may hold values from -0.109375 to 0.109375
- w_gate_up: bfloat16 [8, 2, 2880, 2880], P('ctx', None, None, 'head'), may hold values from -0.109375 to 0.109375
- w_down: bfloat16 [8, 2880, 2880], P('ctx', 'head'), may hold values from -0.109375 to 0.109375
Outputs:
- layer_out: bfloat16 [2048, 2880], P(('group', 'ctx', 'head')), parts along dimension 0
There are 2 independent parts, one for each index of `group`. A program takes and returns all parts, laid end to end along the dimension named above; an argument that names none is the same for every part. Nothing has to cross between parts.
Inputs may be any that keep to these rules, and one draw needn't show every extreme that they name: `routes`: each row names 4 different experts; in each aligned block of 64 rows no expert is named by more than 48 rows, a bound that some block reaches. `segments`: requests fill consecutive positions in order; the longest has 768 positions.
All inputs are finite; a program needn't handle non-finite values.
Results may differ from a plain program's by a relative error of at most 0.015.
Values may be sent and summed in bfloat16 or wider, within the bound.
No kernel may reach another device: no remote copies, remote signals or barrier semaphores. Data moves between devices by JAX's collectives and lax.ppermute only.
A program may use at most 128 MiB of HBM per device.

v0:
```python
import functools

import jax
import jax.numpy as jnp
from jax import lax
from jax.experimental import pallas as pl
from jax.experimental.pallas import tpu as pltpu
from jax.sharding import PartitionSpec as P

HEAD_SIZE = 64
LANES = 128
CORES = 2
VMEM_LIMIT = 16 << 20
STACKED_HEADS = 4
UNIT_PARTS = 3
BF16_ROWS = 16
COLUMNS = 6 * LANES

masked_value = -1e30
NT = (((1,), (1,)), ((), ()))
NN = (((1,), (0,)), ((), ()))


def dot(a, b, dims):
    return lax.dot_general(a, b, dims, preferred_element_type=jnp.float32)


def load_kernel(n, *refs):
    sources, targets, flag, arrived = refs[:n], refs[-n - 2 : -2], refs[-2], refs[-1]
    flag[...] = jnp.zeros(flag.shape, flag.dtype)
    copies = [pltpu.make_async_copy(sources[i], targets[i], arrived.at[i]) for i in range(n)]
    for copy in copies:
        copy.start()
    for copy in copies:
        copy.wait()


def load(arrays, earlier):
    n = len(arrays)
    return pl.pallas_call(
        functools.partial(load_kernel, n),
        out_shape=[pltpu.VMEM(a.shape, a.dtype) for a in arrays]
        + [jax.ShapeDtypeStruct((8, LANES), jnp.float32)],
        in_specs=[pl.BlockSpec(memory_space=pl.ANY)] * n
        + [pl.BlockSpec(memory_space=pltpu.VMEM)],
        out_specs=[pl.BlockSpec(memory_space=pltpu.VMEM)] * (n + 1),
        scratch_shapes=[pltpu.SemaphoreType.DMA((n,))],
        compiler_params=pltpu.CompilerParams(vmem_limit_bytes=VMEM_LIMIT),
        cost_estimate=pl.CostEstimate(
            flops=0, bytes_accessed=sum(4 * a.size for a in arrays), transcendentals=0
        ),
        name="load",
    )(*[in_hbm(a) for a in arrays], earlier)


def in_hbm(x):
    return pltpu.with_memory_space_constraint(x, pltpu.HBM)


def in_vmem(x):
    return pltpu.with_memory_space_constraint(x, pltpu.VMEM)


def pack_kernel(left, right, both, arrived):
    half = left.shape[1]
    if half % LANES:
        both[:, :half] = left[...]
        both[:, half:] = right[...]
        return
    copies = [
        pltpu.make_async_copy(left, both.at[:, pl.ds(0, half)], arrived.at[0]),
        pltpu.make_async_copy(right, both.at[:, pl.ds(half, half)], arrived.at[1]),
    ]
    for copy in copies:
        copy.start()
    for copy in copies:
        copy.wait()


def side_by_side(left, right):
    rows, half = left.shape
    vmem = pl.BlockSpec(memory_space=pltpu.VMEM)
    source = vmem if half % LANES else pl.BlockSpec(memory_space=pl.ANY)
    return pl.pallas_call(
        pack_kernel,
        out_shape=jax.ShapeDtypeStruct((rows, 2 * half), left.dtype),
        in_specs=[source] * 2,
        out_specs=vmem,
        scratch_shapes=[pltpu.SemaphoreType.DMA((2,))],
        compiler_params=pltpu.CompilerParams(vmem_limit_bytes=VMEM_LIMIT),
        cost_estimate=pl.CostEstimate(
            flops=0, bytes_accessed=8 * rows * half, transcendentals=0
        ),
        name="side_by_side",
    )(*[x if half % LANES else in_hbm(x) for x in (left, right)])


def prepare_kernel(place, q_ref, tok_seg, segments, q_out, bias):
    tok_count = q_ref.shape[0]
    for h in range(q_ref.shape[1] // HEAD_SIZE):
        q_out[h * tok_count : (h + 1) * tok_count, :] = q_ref[
            :, h * HEAD_SIZE : (h + 1) * HEAD_SIZE
        ] * jnp.asarray(HEAD_SIZE**-0.5, q_ref.dtype)
    ctx = place[0]
    z_here = ctx // CORES
    core = ctx - z_here * CORES
    first = jnp.sum((segments[...] < tok_seg[...]).astype(jnp.float32), axis=1, keepdims=True)
    tok = ctx * tok_count + lax.broadcasted_iota(jnp.int32, bias.shape, 0)
    lane = lax.broadcasted_iota(jnp.int32, bias.shape, 1)
    block = lane // tok_count
    hop = block // CORES
    owner = (z_here - hop) * CORES + jnp.where(block == hop * CORES, core, 1 - core)
    pos = owner * tok_count + (lane - block * tok_count)
    seen = (z_here >= hop) & (pos <= tok) & (pos.astype(jnp.float32) >= first)
    bias[...] = jnp.where(seen, 0.0, masked_value)


def prepare(place, q, tok_seg, segments):
    tok_count, columns = q.shape
    vmem = pl.BlockSpec(memory_space=pltpu.VMEM)
    return pl.pallas_call(
        prepare_kernel,
        out_shape=[
            jax.ShapeDtypeStruct((columns // HEAD_SIZE * tok_count, HEAD_SIZE), q.dtype),
            jax.ShapeDtypeStruct((tok_count, segments.shape[1]), jnp.float32),
        ],
        in_specs=[pl.BlockSpec(memory_space=pltpu.SMEM)] + [vmem] * 3,
        out_specs=[vmem] * 2,
        compiler_params=pltpu.CompilerParams(vmem_limit_bytes=VMEM_LIMIT),
        cost_estimate=pl.CostEstimate(
            flops=20 * tok_count * segments.shape[1],
            bytes_accessed=4 * tok_count * segments.shape[1],
            transcendentals=0,
        ),
        name="prepare",
    )(place, q, tok_seg, segments)


def attend_kernel(n_ctx, n_head, place, sinks, q_ref, bias, w_ref, *rest):
    kv_refs, rest = rest[:n_ctx], rest[n_ctx:]
    outs, (probs, attended, ordered, weights, arrived) = rest[:n_head], rest[n_head:]
    features = weights.shape[0]
    blocks = [(i, min(features, i + COLUMNS)) for i in range(0, features, COLUMNS)]
    copies = [
        pltpu.make_async_copy(
            w_ref.at[pl.ds(i, end - i)], weights.at[pl.ds(i, end - i)], arrived.at[n]
        )
        for n, (i, end) in enumerate(blocks)
    ]
    for copy in copies:
        copy.start()
    tok_count = bias.shape[0]
    own_rows = tok_count // n_head
    kv_width = kv_refs[0].shape[1] // 2
    kv_groups = kv_width // HEAD_SIZE
    share = q_ref.shape[0] // tok_count // kv_groups
    stack = min(share, STACKED_HEADS)
    for g in range(kv_groups):
        ks = slice(g * HEAD_SIZE, (g + 1) * HEAD_SIZE)
        vs = slice(kv_width + g * HEAD_SIZE, kv_width + (g + 1) * HEAD_SIZE)
        k = jnp.concatenate([ref[:, ks] for ref in kv_refs])
        v = jnp.concatenate([ref[:, vs] for ref in kv_refs])
        for j in range(0, share, stack):
            heads = range(g * share + j, g * share + min(share, j + stack))
            scores = dot(q_ref[heads[0] * tok_count : (heads[-1] + 1) * tok_count, :], k, NT)
            denoms = []
            for i, h in enumerate(heads):
                score = scores[i * tok_count : (i + 1) * tok_count] + bias[...]
                top = jnp.maximum(jnp.max(score, axis=1, keepdims=True), sinks[h])
                prob = jnp.exp(score - top)
                denoms.append(jnp.sum(prob, axis=1, keepdims=True) + jnp.exp(sinks[h] - top))
                probs[(j + i) * tok_count : (j + i + 1) * tok_count, :] = prob.astype(jnp.bfloat16)
            out = dot(probs[j * tok_count : (j + len(heads)) * tok_count, :], v, NN)
            for i, h in enumerate(heads):
                attended[:, h * HEAD_SIZE : (h + 1) * HEAD_SIZE] = (
                    out[i * tok_count : (i + 1) * tok_count] / denoms[i]
                ).astype(jnp.bfloat16)
    head = place[1]
    for j in range(n_head):
        source = lax.rem(head + n_head - j, n_head) * own_rows
        ordered[j * own_rows : (j + 1) * own_rows, :] = attended[
            pl.ds(pl.multiple_of(source, own_rows), own_rows), :
        ]
    width = outs[0].shape[1]
    for out in outs:
        out[:, width - LANES :] = jnp.zeros((own_rows, LANES), out.dtype)
    for copy, (i, end) in zip(copies, blocks):
        copy.wait()
        part = dot(ordered[...], weights[i:end, :], NT).astype(jnp.bfloat16)
        for j in range(n_head):
            outs[j][:, i:end] = part[j * own_rows : (j + 1) * own_rows]


def attend(place, sinks, q, bias, w_out_t, kv, n_head, width):
    tok_count, n_keys = bias.shape
    features, columns = w_out_t.shape
    own_rows = tok_count // n_head
    vmem = pl.BlockSpec(memory_space=pltpu.VMEM)
    smem = pl.BlockSpec(memory_space=pltpu.SMEM)
    share = columns // (kv[0].shape[1] // 2)
    return pl.pallas_call(
        functools.partial(attend_kernel, len(kv), n_head),
        out_shape=[jax.ShapeDtypeStruct((own_rows, width), jnp.bfloat16)] * n_head,
        in_specs=[smem, smem, vmem, vmem, pl.BlockSpec(memory_space=pl.ANY)] + [vmem] * len(kv),
        out_specs=[vmem] * n_head,
        scratch_shapes=[
            pltpu.VMEM((share * tok_count, n_keys), jnp.bfloat16),
            pltpu.VMEM((tok_count, columns), jnp.bfloat16),
            pltpu.VMEM((tok_count, columns), jnp.bfloat16),
            pltpu.VMEM(w_out_t.shape, w_out_t.dtype),
            pltpu.SemaphoreType.DMA((-(-features // COLUMNS),)),
        ],
        compiler_params=pltpu.CompilerParams(vmem_limit_bytes=2 * VMEM_LIMIT),
        cost_estimate=pl.CostEstimate(
            flops=4 * tok_count * columns * n_keys + 2 * tok_count * columns * features,
            bytes_accessed=2 * columns * features,
            transcendentals=tok_count * n_keys * columns // HEAD_SIZE,
        ),
        name="attend",
    )(place, sinks, q, bias, in_hbm(w_out_t), *kv)


def norm_kernel(experts, hidden, routes, gain, router, *refs):
    sums, (residual_out, rows_out) = refs[:-2], refs[-2:]
    features = gain.shape[1]
    total = sums[0][...].astype(jnp.float32)
    for other in sums[1:]:
        total = total + other[...].astype(jnp.float32)
    residual = (hidden[...].astype(jnp.float32) + total).astype(jnp.bfloat16)
    residual_out[...] = residual
    widened = residual[:, :features].astype(jnp.float32)
    scale_rows = lax.rsqrt(jnp.mean(widened * widened, axis=-1, keepdims=True) + 1e-05)
    normed = (widened * scale_rows * gain[...]).astype(jnp.bfloat16)
    logits = dot(normed, router[...], NT)
    tail = rows_out.shape[1] - LANES
    offset = features - tail
    lane = lax.broadcasted_iota(jnp.int32, logits.shape, 1)
    expert = lane - offset
    expert = jnp.where(expert >= experts, expert - experts, expert)
    named = routes[:, 0:1] == expert
    for k in range(1, routes.shape[1]):
        named = named | (routes[:, k : k + 1] == expert)
    high_lanes = (lane >= offset) & (lane < offset + experts)
    low_lanes = (lane >= offset + experts) & (lane < offset + 2 * experts)
    chosen = jnp.where(named & (high_lanes | low_lanes), logits, masked_value)
    top = jnp.max(chosen, axis=1, keepdims=True)
    weight = jnp.exp(chosen - top)
    denom = jnp.sum(jnp.where(high_lanes, weight, 0.0), axis=1, keepdims=True)
    gates = weight / denom
    high = gates.astype(jnp.bfloat16).astype(jnp.float32)
    packed = jnp.where(high_lanes, high, jnp.where(low_lanes, gates - high, 0.0))
    rows_out[:, :features] = normed
    end = rows_out[:, tail:].astype(jnp.float32)
    rows_out[:, tail:] = jnp.where(lane < offset, end, packed).astype(jnp.bfloat16)


def norm_and_gates(sums, hidden, routes, gain, router_lanes, experts):
    rows, width = hidden.shape
    features = gain.shape[1]
    vmem = pl.BlockSpec(memory_space=pltpu.VMEM)
    return pl.pallas_call(
        functools.partial(norm_kernel, experts),
        out_shape=[jax.ShapeDtypeStruct((rows, width), jnp.bfloat16)] * 2,
        in_specs=[vmem] * (4 + len(sums)),
        out_specs=[vmem] * 2,
        compiler_params=pltpu.CompilerParams(vmem_limit_bytes=VMEM_LIMIT),
        cost_estimate=pl.CostEstimate(
            flops=rows * features * LANES * 2,
            bytes_accessed=rows * features * 10,
            transcendentals=rows * LANES,
        ),
        name="norm_and_gates",
    )(hidden, routes, gain, router_lanes, *sums)


def expert_kernel(experts, n_head, place, gate_up, down, flag, *refs):
    near, far = refs[:n_head], refs[n_head : 2 * n_head]
    outs, (far_out, done, rows, hidden) = refs[2 * n_head : -4], refs[-4:]
    done[...] = flag[...]
    units, features = down.shape
    count, width = near[0].shape
    tail = width - LANES
    lane = lax.broadcasted_iota(jnp.int32, (count, LANES), 1) - (features - tail)
    mine = (lane == place[0]) | (lane == place[0] + experts)
    gates = []
    for i, ref in enumerate(near + far):
        rows[i * count : (i + 1) * count, :] = ref[:, :features]
        packed = ref[:, tail:].astype(jnp.float32)
        gates.append(jnp.sum(jnp.where(mine, packed, 0.0), axis=1, keepdims=True))
    for ref in (*outs, far_out):
        ref[:, tail:] = jnp.zeros((ref.shape[0], LANES), ref.dtype)
    parts, _, block = hidden.shape

    def some_units(n, carry):
        here = pl.ds(pl.multiple_of(n * block, BF16_ROWS), block) if parts > 1 else slice(None)
        gate_pre = dot(rows[...], gate_up[0, here, :], NT)
        up_pre = dot(rows[...], gate_up[1, here, :], NT)
        act = gate_pre * jax.nn.sigmoid(1.702 * gate_pre) * (up_pre + 1.0)
        hidden[n] = act.astype(jnp.bfloat16)
        return carry

    lax.fori_loop(0, parts, some_units, 0)
    units_by_row = jnp.concatenate([hidden[n] for n in range(parts)], axis=1)
    for i in range(0, features, COLUMNS):
        end = min(features, i + COLUMNS)
        part = dot(units_by_row, down[:, i:end], NN)
        for j in range(2 * n_head):
            block = (part[j * count : (j + 1) * count] * gates[j]).astype(jnp.bfloat16)
            if j < n_head:
                outs[j][:, i:end] = block
            else:
                far_out[(j - n_head) * count : (j - n_head + 1) * count, i:end] = block


def expert_rows(
                place, near, far, gate_up_t, down, flag, experts
            ):
    count, width = near[0].shape
    units, features = down.shape
    n_head = len(near)
    parts = UNIT_PARTS if units % (UNIT_PARTS * BF16_ROWS) == 0 else 1
    vmem = pl.BlockSpec(memory_space=pltpu.VMEM)
    return pl.pallas_call(
        functools.partial(expert_kernel, experts, n_head),
        out_shape=[jax.ShapeDtypeStruct((count, width), jnp.bfloat16)] * n_head
        + [jax.ShapeDtypeStruct((n_head * count, width), jnp.bfloat16)]
        + [jax.ShapeDtypeStruct(flag.shape, flag.dtype)],
        in_specs=[pl.BlockSpec(memory_space=pltpu.SMEM)] + [vmem] * (3 + 2 * n_head),
        out_specs=[vmem] * (n_head + 2),
        scratch_shapes=[
            pltpu.VMEM((2 * n_head * count, features), jnp.bfloat16),
            pltpu.VMEM((parts, 2 * n_head * count, units // parts), jnp.bfloat16),
        ],
        compiler_params=pltpu.CompilerParams(vmem_limit_bytes=VMEM_LIMIT),
        cost_estimate=pl.CostEstimate(
            flops=12 * n_head * count * units * features,
            bytes_accessed=6 * units * features,
            transcendentals=2 * n_head * count * units,
        ),
        name="expert_rows",
    )(place, in_vmem(gate_up_t), in_vmem(down), flag, *near, *far)


def finish_kernel(n_halves, flag, *refs):
    terms, halves, out = refs[: len(refs) - 1 - n_halves], refs[len(refs) - 1 - n_halves : -1], refs[-1]
    features = out.shape[1]
    start = 0
    for half in halves or terms[:1]:
        end = min(features, start + half.shape[1])
        total = half[:, : end - start].astype(jnp.float32)
        for term in terms if halves else terms[1:]:
            total = total + term[:, start:end].astype(jnp.float32)
        out[:, start:end] = total.astype(out.dtype)
        start = end


def finish(flag, terms, halves, features):
    vmem = pl.BlockSpec(memory_space=pltpu.VMEM)
    rows, width = terms[0].shape
    return pl.pallas_call(
        functools.partial(finish_kernel, len(halves)),
        out_shape=jax.ShapeDtypeStruct((rows, features), terms[0].dtype),
        in_specs=[vmem] * (1 + len(terms) + len(halves)),
        out_specs=vmem,
        compiler_params=pltpu.CompilerParams(vmem_limit_bytes=VMEM_LIMIT),
        cost_estimate=pl.CostEstimate(
            flops=rows * width * (len(terms) + 1),
            bytes_accessed=rows * width * 2 * (len(terms) + 2),
            transcendentals=0,
        ),
        name="finish",
    )(flag, *terms, *halves)


def body(
    queries,
    keys,
    values,
    sinks,
    segments,
    hidden_in,
    routes,
    w_out,
    norm_gain,
    router,
    w_gate_up,
    w_down,
):
    n_ctx = lax.axis_size("ctx")
    n_head = lax.axis_size("head")
    n_z = n_ctx // CORES
    ctx = lax.axis_index("ctx")
    head = lax.axis_index("head")
    tok_count = queries.shape[0]
    features = hidden_in.shape[1]
    experts = router.shape[1]
    own_rows = tok_count // n_head
    width = -(-(features + 2 * experts) // LANES) * LANES

    to_sibling = [(i, i ^ 1) for i in range(n_ctx)]
    ring = list(range(0, n_z, 2))
    ring = ring[::-1] + list(range(1, n_z, 2))
    follower = {ring[i]: ring[(i + 1) % n_z] for i in range(n_z)}
    to_next_chip = [(i, follower[i // CORES] * CORES + i % CORES) for i in range(n_ctx)]

    def sibling(x):
        return lax.ppermute(x, "ctx", to_sibling)

    def next_chip(x):
        return lax.ppermute(x, "ctx", to_next_chip)

    def next_head(x, j):
        return lax.ppermute(x, "head", [(i, (i + j) % n_head) for i in range(n_head)])

    def add(*terms):
        total = terms[0].astype(jnp.float32)
        for term in terms[1:]:
            total = total + term.astype(jnp.float32)
        return total.astype(jnp.bfloat16)

    def after(later, earlier):
        return lax.optimization_barrier((later, earlier))

    place = jnp.stack([ctx, head]).astype(jnp.int32)
    row_start = head * own_rows
    own_hidden = jnp.pad(
        lax.dynamic_slice_in_dim(hidden_in, row_start, own_rows, 0), ((0, 0), (0, width - features))
    )
    own_routes = lax.dynamic_slice_in_dim(routes, row_start, own_rows, 0)
    tok_seg = lax.dynamic_slice_in_dim(segments, ctx * tok_count, tok_count, 0)[:, None]
    tail = features - (width - LANES)
    router_lanes = jnp.pad(
        jnp.concatenate([router.T, router.T]), ((tail, LANES - tail - 2 * experts), (0, 0))
    )

    with jax.named_scope("keys_and_values"):
        own = side_by_side(keys, values)
        kv = [
            lax.ppermute(own, "ctx", [(i, i + CORES * k) for i in range(n_ctx - CORES * k)])
            for k in range(n_z - 1, 0, -1)
        ]
        kv = [own] + kv[::-1]
    with jax.named_scope("attention"):
        q, bias = prepare(place, queries, tok_seg, segments[None, :])
        kv, q = after(kv, q)
        kv = [x for one in kv for x in (one, sibling(one))]
        sums = attend(place, sinks, q, bias, w_out.T, kv, n_head, width)

    with jax.named_scope("norm"):
        gathered = [sums[0]] + [next_head(sums[j], n_head - j) for j in range(1, n_head)]
        down, gate_up_t, flag = load([w_down[0], jnp.swapaxes(w_gate_up[0], 1, 2)], sums[0])
        gathered, flag = after(gathered, flag)
        residual, rows = norm_and_gates(
            gathered, own_hidden, own_routes, norm_gain[None, :], router_lanes, experts
        )

    def to_heads(x):
        return [x] + [next_head(x, j) for j in range(1, n_head)]

    def to_other_heads(sums):
        return [next_head(sums[j - 1], n_head - j) for j in range(1, n_head)]

    with jax.named_scope("rows_of_chips"):
        near = to_heads(rows)
        chunk = next_chip(rows)
        near, chunk, flag = lax.optimization_barrier((near, chunk, flag))

    middle = -(-width // LANES // 2) * LANES
    halves = [slice(0, middle), slice(middle, width)]
    waiting, arriving = None, []
    for hop in range(n_z):
        with jax.named_scope("rows_of_chips"):
            lot, coming = None, None
            if hop < n_z - 2 or hop == 0 and n_z > 1:
                lot = to_heads(chunk)
                coming = next_chip(chunk) if hop < n_z - 2 else None
            elif hop == n_z - 2:
                lot = [chunk] + [next_chip(x) for x in near[1:]]
        with jax.named_scope("experts"):
            far = [sibling(x) for x in near]
            *near_out, far_out, flag = expert_rows(
                place, near, far, gate_up_t, down, flag, experts
            )
        with jax.named_scope("sum_back"):
            lot, coming, waiting, arriving, far_out = lax.optimization_barrier(
                (lot, coming, waiting, arriving, far_out)
            )
            if waiting is not None:
                sent = halves if hop == n_z - 1 else [slice(0, width)]
                arriving = [
                    next_chip(add(*[x[:, part] for x in (*waiting, *arriving)])) for part in sent
                ]
            crossed = sibling(far_out)
            blocks = [
                (near_out[j], crossed[j * own_rows : (j + 1) * own_rows]) for j in range(n_head)
            ]
            if hop == 0:
                own_blocks = blocks
            elif hop < n_z - 1:
                leaving = [add(*block) for block in blocks[1:]]
                leaving, flag = after(leaving, flag)
                waiting = [*blocks[0], *to_other_heads(leaving)]
            near, chunk = lot, coming

    with jax.named_scope("sum_back"):
        if n_z > 1:
            others = [[add(*[x[:, half] for x in b]) for b in blocks[1:]] for half in halves]
            crossing = [to_other_heads(x) for x in others]
            crossing[0], own_blocks = after(crossing[0], own_blocks)
            arriving = [
                next_chip(
                    add(*[x[:, half] for x in blocks[0]], *crossing[i], *arriving[i : i + 1])
                )
                for i, half in enumerate(halves)
            ]
        own_sums = to_other_heads([add(*block) for block in own_blocks[1:]])
        return finish(flag, [*own_blocks[0], residual, *own_sums], arriving, features)


def solution(mesh):
    placed = (
        P(("group", "ctx"), "head"),
        P(("group", "ctx"), "head"),
        P(("group", "ctx"), "head"),
        P("head"),
        P("group"),
        P(("group", "ctx"), None),
        P(("group", "ctx"), None),
        P("head", None),
        P(),
        P(),
        P("ctx", None, None, "head"),
        P("ctx", "head", None),
    )
    return jax.shard_map(
        body,
        mesh=mesh,
        in_specs=placed,
        out_specs=P(("group", "ctx", "head"), None),
        check_vma=False,
    )
```

profile of v0, /device:TPU:0, one launch (start us, length us, event | category | flops | bytes accessed | tf_op | source)
XLA Modules:
  0.0 135.0 jit_solution(15818527822695264638)
XLA Ops:
  0.0 1.0 side_by_side.1.rest_0_
  1.0 7.0 %collective-permute-start.2 = (bf16[128,512]{1,0:T(8,128)(2,1)S(1)}, bf16[128,512]{1,0:T(8,128)(2,1)S(1)}, u32[]{:S(2)}, u32[]{:S(2)}) collective-permute-start(bf16[128,512]{1,0:T(8,128)(2,1)S(1)} %side_by_side.1.rest_0_), channel_id=1, source_target_pairs={{0,12},{2,14},{1,13},{3,15},{16,28},{18,30},{17,29},{19,31}} | collective-permute-start | bytes 393224 | tf_op jit(solution)/shard_map/keys_and_values/ppermute | solution.py:439
  7.9 1.3 collective-permute-start.1
  9.2 2.5 %collective-permute-start = (bf16[128,512]{1,0:T(8,128)(2,1)S(1)}, bf16[128,512]{1,0:T(8,128)(2,1)S(1)}, u32[]{:S(2)}, u32[]{:S(2)}) collective-permute-start(bf16[128,512]{1,0:T(8,128)(2,1)S(1)} %side_by_side.1.rest_0_), channel_id=1, source_target_pairs={{0,4},{2,6},{4,8},{6,10},{8,12},{10,14},{1,5},{3,7},{5,9},{7,11},{... | collective-permute-start | bytes 393224 | tf_op jit(solution)/shard_map/keys_and_values/ppermute | solution.py:439
  11.7 0.8 dynamic-slice_bitcast_fusion
  12.7 1.0 copy-done.2
  13.7 0.7 copy-done.3
  14.4 1.2 prepare.1
  15.6 0.7 collective-permute-done.rest_2_
  16.3 0.5 collective-permute-start.4
  16.8 0.5 collective-permute-start.6
  18.4 13.1 %attend.1 = (bf16[64,2944]{1,0:T(8,128)(2,1)S(1)}, bf16[64,2944]{1,0:T(8,128)(2,1)S(1)}) custom-call(s32[2]{0:T(128)S(1)} %pad_add_fusion.place, f32[32]{0:T(128)S(1)} %copy-done.4, bf16[4096,64]{1,0:T(8,128)(2,1)S(1)} %get-tuple-element.71.q_ref, f32[128,1024]{1,0:T(8,128)S(1)} %get-tuple-element.72.bias, bf16[2880,2048]{1,0:T(8,128)(2,1)} %bitcast.13, ...), custom_call_target="tpu_custom_call" | custom-call | flops 2583691264 | bytes 11796480 | tf_op jit(solution)/shard_map/attention/attend/pallas_call | solution.py:201
  31.5 1.6 %collective-permute-start.7 = (bf16[64,2944]{1,0:T(8,128)(2,1)S(1)}, bf16[64,2944]{1,0:T(8,128)(2,1)S(1)}, u32[]{:S(2)}, u32[]{:S(2)}) collective-permute-start(bf16[64,2944]{1,0:T(8,128)(2,1)S(1)} %get-tuple-element.80), channel_id=1, source_target_pairs={{0,1},{1,0},{2,3},{3,2},{4,5},{5,4},{6,7},{7,6},{8,9},{9,8},{10,11... | collective-permute-start | bytes 1130504 | tf_op jit(solution)/shard_map/norm/ppermute | solution.py:413
  33.6 8.3 %load.1 = (bf16[1440,2880]{1,0:T(8,128)(2,1)S(1)}, bf16[2,1440,2880]{2,1,0:T(8,128)(2,1)S(1)}, f32[8,128]{1,0:T(8,128)S(1)}) custom-call(bf16[1440,2880]{1,0:T(8,128)(2,1)} %bitcast.14, bf16[2,1440,2880]{2,1,0:T(8,128)(2,1)} %bitcast.12, bf16[64,2944]{1,0:T(8,128)(2,1)S(1)} %get-tuple-element.82.refs_2_.refs_0_), custom_call_target="tpu_custom_call" | custom-call | bytes 49766400 | tf_op jit(solution)/shard_map/norm/load/pallas_call | solution.py:40
  42.0 0.6 collective-permute-done.7.refs_1_
  42.5 0.8 norm_and_gates.1
  43.3 4.5 %collective-permute-start.9 = (bf16[64,2944]{1,0:T(8,128)(2,1)S(1)}, bf16[64,2944]{1,0:T(8,128)(2,1)S(1)}, u32[]{:S(2)}, u32[]{:S(2)}) collective-permute-start(bf16[64,2944]{1,0:T(8,128)(2,1)S(1)} %get-tuple-element.87.refs_0_), channel_id=1, source_target_pairs={{0,4},{2,6},{4,12},{6,14},{8,0},{10,2},{12,8},{14,10},{1,5},{3,7},... | collective-permute-start | bytes 1130504 | tf_op jit(solution)/shard_map/rows_of_chips/ppermute | solution.py:410
  47.8 1.5 %collective-permute-start.8 = (bf16[64,2944]{1,0:T(8,128)(2,1)S(1)}, bf16[64,2944]{1,0:T(8,128)(2,1)S(1)}, u32[]{:S(2)}, u32[]{:S(2)}) collective-permute-start(bf16[64,2944]{1,0:T(8,128)(2,1)S(1)} %get-tuple-element.87.refs_0_), channel_id=1, source_target_pairs={{0,1},{1,0},{2,3},{3,2},{4,5},{5,4},{6,7},{7,6},{8,9},{9,8},{10,11... | collective-permute-start | bytes 1130504 | tf_op jit(solution)/shard_map/rows_of_chips/ppermute | solution.py:413
  49.2 8.9 %collective-permute-done.9.refs_0_ = bf16[64,2944]{1,0:T(8,128)(2,1)S(1)} collective-permute-done((bf16[64,2944]{1,0:T(8,128)(2,1)S(1)}, bf16[64,2944]{1,0:T(8,128)(2,1)S(1)}, u32[]{:S(2)}, u32[]{:S(2)}) %collective-permute-start.9) | collective-permute-done | bytes 376864 | tf_op jit(solution)/shard_map/rows_of_chips/ppermute | solution.py:410
  58.1 0.5 collective-permute-start.11
  58.8 1.5 %collective-permute-start.12 = (bf16[64,2944]{1,0:T(8,128)(2,1)S(1)}, bf16[64,2944]{1,0:T(8,128)(2,1)S(1)}, u32[]{:S(2)}, u32[]{:S(2)}) collective-permute-start(bf16[64,2944]{1,0:T(8,128)(2,1)S(1)} %collective-permute-done.9.refs_0_), channel_id=1, source_target_pairs={{0,1},{1,0},{2,3},{3,2},{4,5},{5,4},{6,7},{7,6},{8,9},{9,8},{10,11... | collective-permute-start | bytes 1130504 | tf_op jit(solution)/shard_map/rows_of_chips/ppermute | solution.py:413
  60.4 8.8 %expert_rows.4 = (bf16[64,2944]{1,0:T(8,128)(2,1)S(1)}, bf16[64,2944]{1,0:T(8,128)(2,1)S(1)}, bf16[128,2944]{1,0:T(8,128)(2,1)S(1)}, f32[8,128]{1,0:T(8,128)S(1)}) custom-call(s32[2]{0:T(128)S(1)} %pad_add_fusion.place, bf16[2,1440,2880]{2,1,0:T(8,128)(2,1)S(1)} %get-tuple-element.78.gate_up, bf16[1440,2880]{1,0:T(8,128)(2,1)S(1)} %get-tuple-element.79.down, ...), custom_call_target="tpu_custom_call" | custom-call | flops 6370099200 | bytes 24883200 | tf_op jit(solution)/shard_map/experts/expert_rows/pallas_call | solution.py:323
  69.1 1.1 collective-permute-done.13.refs_0_
  70.2 0.5 collective-permute-start.15
  70.7 2.3 %collective-permute-start.17 = (bf16[64,2944]{1,0:T(8,128)(2,1)S(1)}, bf16[64,2944]{1,0:T(8,128)(2,1)S(1)}, u32[]{:S(2)}, u32[]{:S(2)}) collective-permute-start(bf16[64,2944]{1,0:T(8,128)(2,1)S(1)} %collective-permute-done.13.refs_0_), channel_id=1, source_target_pairs={{0,4},{2,6},{4,12},{6,14},{8,0},{10,2},{12,8},{14,10},{1,5},{3,7},... | collective-permute-start | bytes 1130504 | tf_op jit(solution)/shard_map/rows_of_chips/ppermute | solution.py:410
  73.0 1.5 %collective-permute-start.16 = (bf16[64,2944]{1,0:T(8,128)(2,1)S(1)}, bf16[64,2944]{1,0:T(8,128)(2,1)S(1)}, u32[]{:S(2)}, u32[]{:S(2)}) collective-permute-start(bf16[64,2944]{1,0:T(8,128)(2,1)S(1)} %collective-permute-done.13.refs_0_), channel_id=1, source_target_pairs={{0,1},{1,0},{2,3},{3,2},{4,5},{5,4},{6,7},{7,6},{8,9},{9,8},{10,11... | collective-permute-start | bytes 1130504 | tf_op jit(solution)/shard_map/rows_of_chips/ppermute | solution.py:413
  74.6 8.8 %expert_rows.5 = (bf16[64,2944]{1,0:T(8,128)(2,1)S(1)}, bf16[64,2944]{1,0:T(8,128)(2,1)S(1)}, bf16[128,2944]{1,0:T(8,128)(2,1)S(1)}, f32[8,128]{1,0:T(8,128)S(1)}) custom-call(s32[2]{0:T(128)S(1)} %pad_add_fusion.place, bf16[2,1440,2880]{2,1,0:T(8,128)(2,1)S(1)} %get-tuple-element.78.gate_up, bf16[1440,2880]{1,0:T(8,128)(2,1)S(1)} %get-tuple-element.79.down, ...), custom_call_target="tpu_custom_call" | custom-call | flops 6370099200 | bytes 24883200 | tf_op jit(solution)/shard_map/experts/expert_rows/pallas_call | solution.py:323
  83.5 0.5 collective-permute-start.30
  84.0 1.1 collective-permute-start.21
  85.1 0.5 collective-permute-start.19
  85.8 1.5 %collective-permute-start.22 = (bf16[64,2944]{1,0:T(8,128)(2,1)S(1)}, bf16[64,2944]{1,0:T(8,128)(2,1)S(1)}, u32[]{:S(2)}, u32[]{:S(2)}) collective-permute-start(bf16[64,2944]{1,0:T(8,128)(2,1)S(1)} %add_convert_fusion.3), channel_id=1, source_target_pairs={{0,1},{1,0},{2,3},{3,2},{4,5},{5,4},{6,7},{7,6},{8,9},{9,8},{10,11... | collective-permute-start | bytes 1130504 | tf_op jit(solution)/shard_map/sum_back/ppermute | solution.py:413
  87.3 0.6 collective-permute-done.19.refs_2_
  87.9 8.8 %expert_rows.6 = (bf16[64,2944]{1,0:T(8,128)(2,1)S(1)}, bf16[64,2944]{1,0:T(8,128)(2,1)S(1)}, bf16[128,2944]{1,0:T(8,128)(2,1)S(1)}, f32[8,128]{1,0:T(8,128)S(1)}) custom-call(s32[2]{0:T(128)S(1)} %pad_add_fusion.place, bf16[2,1440,2880]{2,1,0:T(8,128)(2,1)S(1)} %get-tuple-element.78.gate_up, bf16[1440,2880]{1,0:T(8,128)(2,1)S(1)} %get-tuple-element.79.down, ...), custom_call_target="tpu_custom_call" | custom-call | flops 6370099200 | bytes 24883200 | tf_op jit(solution)/shard_map/experts/expert_rows/pallas_call | solution.py:323
  97.0 0.7 slice-done
  97.8 1.2 collective-permute-start.27
  99.0 0.5 collective-permute-start.25
  99.6 1.6 %collective-permute-start.26 = (bf16[64,2944]{1,0:T(8,128)(2,1)S(1)}, bf16[64,2944]{1,0:T(8,128)(2,1)S(1)}, u32[]{:S(2)}, u32[]{:S(2)}) collective-permute-start(bf16[64,2944]{1,0:T(8,128)(2,1)S(1)} %add_convert_fusion.2), channel_id=1, source_target_pairs={{0,1},{1,0},{2,3},{3,2},{4,5},{5,4},{6,7},{7,6},{8,9},{9,8},{10,11... | collective-permute-start | bytes 1130504 | tf_op jit(solution)/shard_map/sum_back/ppermute | solution.py:413
  101.3 8.8 %expert_rows.7 = (bf16[64,2944]{1,0:T(8,128)(2,1)S(1)}, bf16[64,2944]{1,0:T(8,128)(2,1)S(1)}, bf16[128,2944]{1,0:T(8,128)(2,1)S(1)}, f32[8,128]{1,0:T(8,128)S(1)}) custom-call(s32[2]{0:T(128)S(1)} %pad_add_fusion.place, bf16[2,1440,2880]{2,1,0:T(8,128)(2,1)S(1)} %get-tuple-element.78.gate_up, bf16[1440,2880]{1,0:T(8,128)(2,1)S(1)} %get-tuple-element.79.down, ...), custom_call_target="tpu_custom_call" | custom-call | flops 6370099200 | bytes 24883200 | tf_op jit(solution)/shard_map/experts/expert_rows/pallas_call | solution.py:323
  110.5 1.2 collective-permute-start.35
  111.8 1.1 collective-permute-start.32
  112.9 1.5 %collective-permute-start.29 = (bf16[64,1536]{1,0:T(8,128)(2,1)S(1)}, bf16[64,1536]{1,0:T(8,128)(2,1)S(1)}, u32[]{:S(2)}, u32[]{:S(2)}) collective-permute-start(bf16[64,1536]{1,0:T(8,128)(2,1)S(1)} %add_convert_fusion.6), channel_id=1, source_target_pairs={{0,1},{1,0},{2,3},{3,2},{4,5},{5,4},{6,7},{7,6},{8,9},{9,8},{10,11... | collective-permute-start | bytes 589832 | tf_op jit(solution)/shard_map/sum_back/ppermute | solution.py:413
  114.5 0.6 collective-permute-start.34
  115.1 5.6 %collective-permute-done.29 = bf16[64,1536]{1,0:T(8,128)(2,1)S(1)} collective-permute-done((bf16[64,1536]{1,0:T(8,128)(2,1)S(1)}, bf16[64,1536]{1,0:T(8,128)(2,1)S(1)}, u32[]{:S(2)}, u32[]{:S(2)}) %collective-permute-start.29) | collective-permute-done | bytes 196640 | tf_op jit(solution)/shard_map/sum_back/ppermute | solution.py:413
  120.8 1.8 %collective-permute-done.32 = bf16[64,1536]{1,0:T(8,128)(2,1)S(1)} collective-permute-done((bf16[64,1536]{1,0:T(8,128)(2,1)S(1)}, bf16[64,1536]{1,0:T(8,128)(2,1)S(1)}, u32[]{:S(2)}, u32[]{:S(2)}) %collective-permute-start.32) | collective-permute-done | bytes 196640 | tf_op jit(solution)/shard_map/sum_back/ppermute | solution.py:410
  123.1 1.6 %collective-permute-start.31 = (bf16[64,2944]{1,0:T(8,128)(2,1)S(1)}, bf16[64,2944]{1,0:T(8,128)(2,1)S(1)}, u32[]{:S(2)}, u32[]{:S(2)}) collective-permute-start(bf16[64,2944]{1,0:T(8,128)(2,1)S(1)} %add_convert_fusion), channel_id=1, source_target_pairs={{0,1},{1,0},{2,3},{3,2},{4,5},{5,4},{6,7},{7,6},{8,9},{9,8},{10,11... | collective-permute-start | bytes 1130504 | tf_op jit(solution)/shard_map/sum_back/ppermute | solution.py:413
  124.8 1.9 %collective-permute-start.36 = (bf16[64,1408]{1,0:T(8,128)(2,1)S(1)}, bf16[64,1408]{1,0:T(8,128)(2,1)S(1)}, u32[]{:S(2)}, u32[]{:S(2)}) collective-permute-start(bf16[64,1408]{1,0:T(8,128)(2,1)S(1)} %add_convert_fusion.7), channel_id=1, source_target_pairs={{0,4},{2,6},{4,12},{6,14},{8,0},{10,2},{12,8},{14,10},{1,5},{3,7},... | collective-permute-start | bytes 540680 | tf_op jit(solution)/shard_map/sum_back/ppermute | solution.py:410
  126.7 7.3 %collective-permute-done.36.refs_5_ = bf16[64,1408]{1,0:T(8,128)(2,1)S(1)} collective-permute-done((bf16[64,1408]{1,0:T(8,128)(2,1)S(1)}, bf16[64,1408]{1,0:T(8,128)(2,1)S(1)}, u32[]{:S(2)}, u32[]{:S(2)}) %collective-permute-start.36) | collective-permute-done | bytes 180256 | tf_op jit(solution)/shard_map/sum_back/ppermute | solution.py:410
  134.0 1.0 finish.1
  (78 shorter events, 4.2 us)
Async XLA Ops:
  0.0 17.4 %copy-start = (bf16[128,2880]{0,1:T(8,128)(2,1)S(1)}, bf16[128,2880]{0,1:T(8,128)(2,1)}, u32[]{:S(2)}) copy-start(bf16[128,2880]{0,1:T(8,128)(2,1)} %param.17) | copy-start | bytes 2211844
  0.0 18.4 %copy-start.4 = (f32[32]{0:T(128)S(1)}, f32[32]{0:T(128)}, u32[]{:S(2)}) copy-start(f32[32]{0:T(128)} %sinks.1) | copy-start | bytes 388
  1.0 14.6 %collective-permute-start.2 = (bf16[128,512]{1,0:T(8,128)(2,1)S(1)}, bf16[128,512]{1,0:T(8,128)(2,1)S(1)}, u32[]{:S(2)}, u32[]{:S(2)}) collective-permute-start(bf16[128,512]{1,0:T(8,128)(2,1)S(1)} %side_by_side.1.rest_0_), channel_id=1, source_target_pairs={{0,12},{2,14},{1,13},{3,15},{16,28},{18,30},{17,29},{19,31}} | collective-permute-start | bytes 393224 | tf_op jit(solution)/shard_map/keys_and_values/ppermute | solution.py:439
  7.9 7.7 %collective-permute-start.1 = (bf16[128,512]{1,0:T(8,128)(2,1)S(1)}, bf16[128,512]{1,0:T(8,128)(2,1)S(1)}, u32[]{:S(2)}, u32[]{:S(2)}) collective-permute-start(bf16[128,512]{1,0:T(8,128)(2,1)S(1)} %side_by_side.1.rest_0_), channel_id=1, source_target_pairs={{0,8},{2,10},{4,12},{6,14},{1,9},{3,11},{5,13},{7,15},{16,24},{18,... | collective-permute-start | bytes 393224 | tf_op jit(solution)/shard_map/keys_and_values/ppermute | solution.py:439
  9.2 7.1 %collective-permute-start = (bf16[128,512]{1,0:T(8,128)(2,1)S(1)}, bf16[128,512]{1,0:T(8,128)(2,1)S(1)}, u32[]{:S(2)}, u32[]{:S(2)}) collective-permute-start(bf16[128,512]{1,0:T(8,128)(2,1)S(1)} %side_by_side.1.rest_0_), channel_id=1, source_target_pairs={{0,4},{2,6},{4,8},{6,10},{8,12},{10,14},{1,5},{3,7},{5,9},{7,11},{... | collective-permute-start | bytes 393224 | tf_op jit(solution)/shard_map/keys_and_values/ppermute | solution.py:439
  12.7 1.0 copy-start.2
  13.7 0.7 copy-start.3
  16.3 1.3 collective-permute-start.3
  16.3 1.5 %collective-permute-start.4 = (bf16[128,512]{1,0:T(8,128)(2,1)S(1)}, bf16[128,512]{1,0:T(8,128)(2,1)S(1)}, u32[]{:S(2)}, u32[]{:S(2)}) collective-permute-start(bf16[128,512]{1,0:T(8,128)(2,1)S(1)} %collective-permute-done.rest_2_), channel_id=1, source_target_pairs={{0,2},{2,0},{4,6},{6,4},{8,10},{10,8},{12,14},{14,12},{1,3},{3,1},... | collective-permute-start | bytes 393224 | tf_op jit(solution)/shard_map/attention/ppermute | solution.py:407
  16.8 1.3 collective-permute-start.5
  16.8 1.5 %collective-permute-start.6 = (bf16[128,512]{1,0:T(8,128)(2,1)S(1)}, bf16[128,512]{1,0:T(8,128)(2,1)S(1)}, u32[]{:S(2)}, u32[]{:S(2)}) collective-permute-start(bf16[128,512]{1,0:T(8,128)(2,1)S(1)} %collective-permute-done.2.rest_6_), channel_id=1, source_target_pairs={{0,2},{2,0},{4,6},{6,4},{8,10},{10,8},{12,14},{14,12},{1,3},{3,1},... | collective-permute-start | bytes 393224 | tf_op jit(solution)/shard_map/attention/ppermute | solution.py:407
  18.4 14.6 %copy-start.8 = (s32[128,4]{0,1:T(4,128)S(1)}, s32[128,4]{0,1:T(4,128)}, u32[]{:S(2)}) copy-start(s32[128,4]{0,1:T(4,128)} %param.18) | copy-start | bytes 6148
  18.4 14.7 %copy-start.7 = (f32[2880]{0:T(1024)S(1)}, f32[2880]{0:T(1024)}, u32[]{:S(2)}) copy-start(f32[2880]{0:T(1024)} %param.20) | copy-start | bytes 34564
  31.4 2.1 %copy-start.6 = (bf16[2880,8]{0,1:T(8,128)(2,1)S(1)}, bf16[2880,8]{0,1:T(8,128)(2,1)}, u32[]{:S(2)}) copy-start(bf16[2880,8]{0,1:T(8,128)(2,1)} %param.21) | copy-start | bytes 138244
  31.5 11.1 %collective-permute-start.7 = (bf16[64,2944]{1,0:T(8,128)(2,1)S(1)}, bf16[64,2944]{1,0:T(8,128)(2,1)S(1)}, u32[]{:S(2)}, u32[]{:S(2)}) collective-permute-start(bf16[64,2944]{1,0:T(8,128)(2,1)S(1)} %get-tuple-element.80), channel_id=1, source_target_pairs={{0,1},{1,0},{2,3},{3,2},{4,5},{5,4},{6,7},{7,6},{8,9},{9,8},{10,11... | collective-permute-start | bytes 1130504 | tf_op jit(solution)/shard_map/norm/ppermute | solution.py:413
  43.3 14.8 %collective-permute-start.9 = (bf16[64,2944]{1,0:T(8,128)(2,1)S(1)}, bf16[64,2944]{1,0:T(8,128)(2,1)S(1)}, u32[]{:S(2)}, u32[]{:S(2)}) collective-permute-start(bf16[64,2944]{1,0:T(8,128)(2,1)S(1)} %get-tuple-element.87.refs_0_), channel_id=1, source_target_pairs={{0,4},{2,6},{4,12},{6,14},{8,0},{10,2},{12,8},{14,10},{1,5},{3,7},... | collective-permute-start | bytes 1130504 | tf_op jit(solution)/shard_map/rows_of_chips/ppermute | solution.py:410
  47.8 10.4 %collective-permute-start.8 = (bf16[64,2944]{1,0:T(8,128)(2,1)S(1)}, bf16[64,2944]{1,0:T(8,128)(2,1)S(1)}, u32[]{:S(2)}, u32[]{:S(2)}) collective-permute-start(bf16[64,2944]{1,0:T(8,128)(2,1)S(1)} %get-tuple-element.87.refs_0_), channel_id=1, source_target_pairs={{0,1},{1,0},{2,3},{3,2},{4,5},{5,4},{6,7},{7,6},{8,9},{9,8},{10,11... | collective-permute-start | bytes 1130504 | tf_op jit(solution)/shard_map/rows_of_chips/ppermute | solution.py:413
  58.1 2.2 %collective-permute-start.10 = (bf16[64,2944]{1,0:T(8,128)(2,1)S(1)}, bf16[64,2944]{1,0:T(8,128)(2,1)S(1)}, u32[]{:S(2)}, u32[]{:S(2)}) collective-permute-start(bf16[64,2944]{1,0:T(8,128)(2,1)S(1)} %get-tuple-element.87.refs_0_), channel_id=1, source_target_pairs={{0,2},{2,0},{4,6},{6,4},{8,10},{10,8},{12,14},{14,12},{1,3},{3,1},... | collective-permute-start | bytes 1130504 | tf_op jit(solution)/shard_map/experts/ppermute | solution.py:407
  58.1 2.2 %collective-permute-start.11 = (bf16[64,2944]{1,0:T(8,128)(2,1)S(1)}, bf16[64,2944]{1,0:T(8,128)(2,1)S(1)}, u32[]{:S(2)}, u32[]{:S(2)}) collective-permute-start(bf16[64,2944]{1,0:T(8,128)(2,1)S(1)} %collective-permute-done.8.refs_1_), channel_id=1, source_target_pairs={{0,2},{2,0},{4,6},{6,4},{8,10},{10,8},{12,14},{14,12},{1,3},{3,1},... | collective-permute-start | bytes 1130504 | tf_op jit(solution)/shard_map/experts/ppermute | solution.py:407
  58.6 11.6 %collective-permute-start.13 = (bf16[64,2944]{1,0:T(8,128)(2,1)S(1)}, bf16[64,2944]{1,0:T(8,128)(2,1)S(1)}, u32[]{:S(2)}, u32[]{:S(2)}) collective-permute-start(bf16[64,2944]{1,0:T(8,128)(2,1)S(1)} %collective-permute-done.9.refs_0_), channel_id=1, source_target_pairs={{0,4},{2,6},{4,12},{6,14},{8,0},{10,2},{12,8},{14,10},{1,5},{3,7},... | collective-permute-start | bytes 1130504 | tf_op jit(solution)/shard_map/rows_of_chips/ppermute | solution.py:410
  58.8 11.4 %collective-permute-start.12 = (bf16[64,2944]{1,0:T(8,128)(2,1)S(1)}, bf16[64,2944]{1,0:T(8,128)(2,1)S(1)}, u32[]{:S(2)}, u32[]{:S(2)}) collective-permute-start(bf16[64,2944]{1,0:T(8,128)(2,1)S(1)} %collective-permute-done.9.refs_0_), channel_id=1, source_target_pairs={{0,1},{1,0},{2,3},{3,2},{4,5},{5,4},{6,7},{7,6},{8,9},{9,8},{10,11... | collective-permute-start | bytes 1130504 | tf_op jit(solution)/shard_map/rows_of_chips/ppermute | solution.py:413
  70.2 4.3 %collective-permute-start.14 = (bf16[64,2944]{1,0:T(8,128)(2,1)S(1)}, bf16[64,2944]{1,0:T(8,128)(2,1)S(1)}, u32[]{:S(2)}, u32[]{:S(2)}) collective-permute-start(bf16[64,2944]{1,0:T(8,128)(2,1)S(1)} %collective-permute-done.9.refs_0_), channel_id=1, source_target_pairs={{0,2},{2,0},{4,6},{6,4},{8,10},{10,8},{12,14},{14,12},{1,3},{3,1},... | collective-permute-start | bytes 1130504 | tf_op jit(solution)/shard_map/experts/ppermute | solution.py:407
  70.2 4.3 %collective-permute-start.15 = (bf16[64,2944]{1,0:T(8,128)(2,1)S(1)}, bf16[64,2944]{1,0:T(8,128)(2,1)S(1)}, u32[]{:S(2)}, u32[]{:S(2)}) collective-permute-start(bf16[64,2944]{1,0:T(8,128)(2,1)S(1)} %collective-permute-done.12.refs_1_), channel_id=1, source_target_pairs={{0,2},{2,0},{4,6},{6,4},{8,10},{10,8},{12,14},{14,12},{1,3},{3,1},... | collective-permute-start | bytes 1130504 | tf_op jit(solution)/shard_map/experts/ppermute | solution.py:407
  70.7 12.6 %collective-permute-start.17 = (bf16[64,2944]{1,0:T(8,128)(2,1)S(1)}, bf16[64,2944]{1,0:T(8,128)(2,1)S(1)}, u32[]{:S(2)}, u32[]{:S(2)}) collective-permute-start(bf16[64,2944]{1,0:T(8,128)(2,1)S(1)} %collective-permute-done.13.refs_0_), channel_id=1, source_target_pairs={{0,4},{2,6},{4,12},{6,14},{8,0},{10,2},{12,8},{14,10},{1,5},{3,7},... | collective-permute-start | bytes 1130504 | tf_op jit(solution)/shard_map/rows_of_chips/ppermute | solution.py:410
  73.0 10.5 %collective-permute-start.16 = (bf16[64,2944]{1,0:T(8,128)(2,1)S(1)}, bf16[64,2944]{1,0:T(8,128)(2,1)S(1)}, u32[]{:S(2)}, u32[]{:S(2)}) collective-permute-start(bf16[64,2944]{1,0:T(8,128)(2,1)S(1)} %collective-permute-done.13.refs_0_), channel_id=1, source_target_pairs={{0,1},{1,0},{2,3},{3,2},{4,5},{5,4},{6,7},{7,6},{8,9},{9,8},{10,11... | collective-permute-start | bytes 1130504 | tf_op jit(solution)/shard_map/rows_of_chips/ppermute | solution.py:413
  83.5 2.2 %collective-permute-start.18 = (bf16[128,2944]{1,0:T(8,128)(2,1)S(1)}, bf16[128,2944]{1,0:T(8,128)(2,1)S(1)}, u32[]{:S(2)}, u32[]{:S(2)}) collective-permute-start(bf16[128,2944]{1,0:T(8,128)(2,1)S(1)} %get-tuple-element.97), channel_id=1, source_target_pairs={{0,2},{2,0},{4,6},{6,4},{8,10},{10,8},{12,14},{14,12},{1,3},{3,1},... | collective-permute-start | bytes 2261000 | tf_op jit(solution)/shard_map/sum_back/ppermute | solution.py:407
  83.5 13.4 %collective-permute-start.30 = (bf16[128,2944]{1,0:T(8,128)(2,1)S(1)}, bf16[128,2944]{1,0:T(8,128)(2,1)S(1)}, u32[]{:S(2)}, u32[]{:S(2)}) collective-permute-start(bf16[128,2944]{1,0:T(8,128)(2,1)S(1)} %get-tuple-element.122), channel_id=1, source_target_pairs={{0,2},{2,0},{4,6},{6,4},{8,10},{10,8},{12,14},{14,12},{1,3},{3,1},... | collective-permute-start | bytes 2261000 | tf_op jit(solution)/shard_map/sum_back/ppermute | solution.py:407
  84.0 12.7 %collective-permute-start.21 = (bf16[64,2944]{1,0:T(8,128)(2,1)S(1)}, bf16[64,2944]{1,0:T(8,128)(2,1)S(1)}, u32[]{:S(2)}, u32[]{:S(2)}) collective-permute-start(bf16[64,2944]{1,0:T(8,128)(2,1)S(1)} %collective-permute-done.16.refs_1_), channel_id=1, source_target_pairs={{0,4},{2,6},{4,12},{6,14},{8,0},{10,2},{12,8},{14,10},{1,5},{3,7},... | collective-permute-start | bytes 1130504 | tf_op jit(solution)/shard_map/rows_of_chips/ppermute | solution.py:410
  85.1 2.8 %collective-permute-start.20 = (bf16[64,2944]{1,0:T(8,128)(2,1)S(1)}, bf16[64,2944]{1,0:T(8,128)(2,1)S(1)}, u32[]{:S(2)}, u32[]{:S(2)}) collective-permute-start(bf16[64,2944]{1,0:T(8,128)(2,1)S(1)} %collective-permute-done.16.refs_1_), channel_id=1, source_target_pairs={{0,2},{2,0},{4,6},{6,4},{8,10},{10,8},{12,14},{14,12},{1,3},{3,1},... | collective-permute-start | bytes 1130504 | tf_op jit(solution)/shard_map/experts/ppermute | solution.py:407
  85.1 2.8 %collective-permute-start.19 = (bf16[64,2944]{1,0:T(8,128)(2,1)S(1)}, bf16[64,2944]{1,0:T(8,128)(2,1)S(1)}, u32[]{:S(2)}, u32[]{:S(2)}) collective-permute-start(bf16[64,2944]{1,0:T(8,128)(2,1)S(1)} %collective-permute-done.13.refs_0_), channel_id=1, source_target_pairs={{0,2},{2,0},{4,6},{6,4},{8,10},{10,8},{12,14},{14,12},{1,3},{3,1},... | collective-permute-start | bytes 1130504 | tf_op jit(solution)/shard_map/experts/ppermute | solution.py:407
  85.7 10.9 %copy-start.5 = (bf16[128,2944]{1,0:T(8,128)(2,1)}, bf16[128,2944]{1,0:T(8,128)(2,1)S(1)}, u32[]{:S(2)}) copy-start(bf16[128,2944]{1,0:T(8,128)(2,1)S(1)} %collective-permute-done.18) | copy-start | bytes 2260996
  85.8 10.9 %collective-permute-start.22 = (bf16[64,2944]{1,0:T(8,128)(2,1)S(1)}, bf16[64,2944]{1,0:T(8,128)(2,1)S(1)}, u32[]{:S(2)}, u32[]{:S(2)}) collective-permute-start(bf16[64,2944]{1,0:T(8,128)(2,1)S(1)} %add_convert_fusion.3), channel_id=1, source_target_pairs={{0,1},{1,0},{2,3},{3,2},{4,5},{5,4},{6,7},{7,6},{8,9},{9,8},{10,11... | collective-permute-start | bytes 1130504 | tf_op jit(solution)/shard_map/sum_back/ppermute | solution.py:413
  96.7 1.0 slice-start
  96.7 2.8 %collective-permute-start.23 = (bf16[128,2944]{1,0:T(8,128)(2,1)S(1)}, bf16[128,2944]{1,0:T(8,128)(2,1)S(1)}, u32[]{:S(2)}, u32[]{:S(2)}) collective-permute-start(bf16[128,2944]{1,0:T(8,128)(2,1)S(1)} %get-tuple-element.107), channel_id=1, source_target_pairs={{0,2},{2,0},{4,6},{6,4},{8,10},{10,8},{12,14},{14,12},{1,3},{3,1},... | collective-permute-start | bytes 2261000 | tf_op jit(solution)/shard_map/sum_back/ppermute | solution.py:407
  97.8 12.2 %collective-permute-start.27 = (bf16[64,2944]{1,0:T(8,128)(2,1)S(1)}, bf16[64,2944]{1,0:T(8,128)(2,1)S(1)}, u32[]{:S(2)}, u32[]{:S(2)}) collective-permute-start(bf16[64,2944]{1,0:T(8,128)(2,1)S(1)} %add_convert_fusion.1), channel_id=1, source_target_pairs={{0,4},{2,6},{4,12},{6,14},{8,0},{10,2},{12,8},{14,10},{1,5},{3,7},... | collective-permute-start | bytes 1130504 | tf_op jit(solution)/shard_map/sum_back/ppermute | solution.py:410
  99.0 2.2 %collective-permute-start.24 = (bf16[64,2944]{1,0:T(8,128)(2,1)S(1)}, bf16[64,2944]{1,0:T(8,128)(2,1)S(1)}, u32[]{:S(2)}, u32[]{:S(2)}) collective-permute-start(bf16[64,2944]{1,0:T(8,128)(2,1)S(1)} %collective-permute-done.17.refs_0_), channel_id=1, source_target_pairs={{0,2},{2,0},{4,6},{6,4},{8,10},{10,8},{12,14},{14,12},{1,3},{3,1},... | collective-permute-start | bytes 1130504 | tf_op jit(solution)/shard_map/experts/ppermute | solution.py:407
  99.0 2.2 %collective-permute-start.25 = (bf16[64,2944]{1,0:T(8,128)(2,1)S(1)}, bf16[64,2944]{1,0:T(8,128)(2,1)S(1)}, u32[]{:S(2)}, u32[]{:S(2)}) collective-permute-start(bf16[64,2944]{1,0:T(8,128)(2,1)S(1)} %collective-permute-done.21.refs_1_), channel_id=1, source_target_pairs={{0,2},{2,0},{4,6},{6,4},{8,10},{10,8},{12,14},{14,12},{1,3},{3,1},... | collective-permute-start | bytes 1130504 | tf_op jit(solution)/shard_map/experts/ppermute | solution.py:407
  99.6 10.7 %collective-permute-start.26 = (bf16[64,2944]{1,0:T(8,128)(2,1)S(1)}, bf16[64,2944]{1,0:T(8,128)(2,1)S(1)}, u32[]{:S(2)}, u32[]{:S(2)}) collective-permute-start(bf16[64,2944]{1,0:T(8,128)(2,1)S(1)} %add_convert_fusion.2), channel_id=1, source_target_pairs={{0,1},{1,0},{2,3},{3,2},{4,5},{5,4},{6,7},{7,6},{8,9},{9,8},{10,11... | collective-permute-start | bytes 1130504 | tf_op jit(solution)/shard_map/sum_back/ppermute | solution.py:413
  110.4 2.5 %collective-permute-start.28 = (bf16[128,2944]{1,0:T(8,128)(2,1)S(1)}, bf16[128,2944]{1,0:T(8,128)(2,1)S(1)}, u32[]{:S(2)}, u32[]{:S(2)}) collective-permute-start(bf16[128,2944]{1,0:T(8,128)(2,1)S(1)} %get-tuple-element.120), channel_id=1, source_target_pairs={{0,2},{2,0},{4,6},{6,4},{8,10},{10,8},{12,14},{14,12},{1,3},{3,1},... | collective-permute-start | bytes 2261000 | tf_op jit(solution)/shard_map/sum_back/ppermute | solution.py:407
  110.5 14.2 %collective-permute-start.35 = (bf16[64,1408]{1,0:T(8,128)(2,1)S(1)}, bf16[64,1408]{1,0:T(8,128)(2,1)S(1)}, u32[]{:S(2)}, u32[]{:S(2)}) collective-permute-start(bf16[64,1408]{1,0:T(8,128)(2,1)S(1)} %add_convert_fusion.8), channel_id=1, source_target_pairs={{0,4},{2,6},{4,12},{6,14},{8,0},{10,2},{12,8},{14,10},{1,5},{3,7},... | collective-permute-start | bytes 540680 | tf_op jit(solution)/shard_map/sum_back/ppermute | solution.py:410
  111.8 10.8 %collective-permute-start.32 = (bf16[64,1536]{1,0:T(8,128)(2,1)S(1)}, bf16[64,1536]{1,0:T(8,128)(2,1)S(1)}, u32[]{:S(2)}, u32[]{:S(2)}) collective-permute-start(bf16[64,1536]{1,0:T(8,128)(2,1)S(1)} %add_convert_fusion.5), channel_id=1, source_target_pairs={{0,4},{2,6},{4,12},{6,14},{8,0},{10,2},{12,8},{14,10},{1,5},{3,7},... | collective-permute-start | bytes 589832 | tf_op jit(solution)/shard_map/sum_back/ppermute | solution.py:410
  112.9 7.8 %collective-permute-start.29 = (bf16[64,1536]{1,0:T(8,128)(2,1)S(1)}, bf16[64,1536]{1,0:T(8,128)(2,1)S(1)}, u32[]{:S(2)}, u32[]{:S(2)}) collective-permute-start(bf16[64,1536]{1,0:T(8,128)(2,1)S(1)} %add_convert_fusion.6), channel_id=1, source_target_pairs={{0,1},{1,0},{2,3},{3,2},{4,5},{5,4},{6,7},{7,6},{8,9},{9,8},{10,11... | collective-permute-start | bytes 589832 | tf_op jit(solution)/shard_map/sum_back/ppermute | solution.py:413
  114.5 10.2 %collective-permute-start.34 = (bf16[64,1408]{1,0:T(8,128)(2,1)S(1)}, bf16[64,1408]{1,0:T(8,128)(2,1)S(1)}, u32[]{:S(2)}, u32[]{:S(2)}) collective-permute-start(bf16[64,1408]{1,0:T(8,128)(2,1)S(1)} %add_convert_fusion.9), channel_id=1, source_target_pairs={{0,1},{1,0},{2,3},{3,2},{4,5},{5,4},{6,7},{7,6},{8,9},{9,8},{10,11... | collective-permute-start | bytes 540680 | tf_op jit(solution)/shard_map/sum_back/ppermute | solution.py:413
  122.7 11.3 %collective-permute-start.33 = (bf16[64,1536]{1,0:T(8,128)(2,1)S(1)}, bf16[64,1536]{1,0:T(8,128)(2,1)S(1)}, u32[]{:S(2)}, u32[]{:S(2)}) collective-permute-start(bf16[64,1536]{1,0:T(8,128)(2,1)S(1)} %add_convert_fusion.4), channel_id=1, source_target_pairs={{0,4},{2,6},{4,12},{6,14},{8,0},{10,2},{12,8},{14,10},{1,5},{3,7},... | collective-permute-start | bytes 589832 | tf_op jit(solution)/shard_map/sum_back/ppermute | solution.py:410
  123.0 12.0 %copy-start.1 = (bf16[128,2880]{0,1:T(8,128)(2,1)S(1)}, bf16[128,2880]{0,1:T(8,128)(2,1)}, u32[]{:S(2)}) copy-start(bf16[128,2880]{0,1:T(8,128)(2,1)} %param.17) | copy-start | bytes 2211844
  123.1 10.9 %collective-permute-start.31 = (bf16[64,2944]{1,0:T(8,128)(2,1)S(1)}, bf16[64,2944]{1,0:T(8,128)(2,1)S(1)}, u32[]{:S(2)}, u32[]{:S(2)}) collective-permute-start(bf16[64,2944]{1,0:T(8,128)(2,1)S(1)} %add_convert_fusion), channel_id=1, source_target_pairs={{0,1},{1,0},{2,3},{3,2},{4,5},{5,4},{6,7},{7,6},{8,9},{9,8},{10,11... | collective-permute-start | bytes 1130504 | tf_op jit(solution)/shard_map/sum_back/ppermute | solution.py:413
  124.8 9.2 %collective-permute-start.36 = (bf16[64,1408]{1,0:T(8,128)(2,1)S(1)}, bf16[64,1408]{1,0:T(8,128)(2,1)S(1)}, u32[]{:S(2)}, u32[]{:S(2)}) collective-permute-start(bf16[64,1408]{1,0:T(8,128)(2,1)S(1)} %add_convert_fusion.7), channel_id=1, source_target_pairs={{0,4},{2,6},{4,12},{6,14},{8,0},{10,2},{12,8},{14,10},{1,5},{3,7},... | collective-permute-start | bytes 540680 | tf_op jit(solution)/shard_map/sum_back/ppermute | solution.py:410
where the time goes:
time: 135 us
  Pallas kernels  60.4 us (45%)
  starting transfers between devices  41.2 us (31%)
  waiting for transfers between devices  28 us (21%)
  local copies, waits for them, and re-layouts  4.2 us (3%)
    pallas_call x4, Pallas kernels, expert_rows(): pl.pallas_call(functools.partial(expert_kernel, experts, n_head), out_sha...  35.1 us
    ppermute x9, waiting for transfers between devices, next_chip(): return lax.ppermute(x, 'ctx', to_next_chip)  19.1 us
    ppermute x9, starting transfers between devices, next_chip(): return lax.ppermute(x, 'ctx', to_next_chip)  13.8 us
    pallas_call x1, Pallas kernels, attend(): pl.pallas_call(functools.partial(attend_kernel, len(kv), n_head), out_sha...  13.1 us
    ppermute x9, starting transfers between devices, next_head(): lax.ppermute(x, 'head', [(i, (i + j) % n_head) for i in range(n_head)])  12.9 us
    ppermute x3, starting transfers between devices, body(): lax.ppermute(own, 'ctx', [(i, i + CORES * k) for i in range(n_ctx - CORES...  10.7 us
    pallas_call x1, Pallas kernels, load(): pl.pallas_call(functools.partial(load_kernel, n), out_shape=[pltpu.VMEM(a...  8.33 us
    ppermute x9, waiting for transfers between devices, next_head(): lax.ppermute(x, 'head', [(i, (i + j) % n_head) for i in range(n_head)])  6.67 us
  transfers between devices with their start and end apart: 37, of which 15 were waited for; matrix products, arithmetic and copies ran while one was open for 2% of the time, Pallas kernels for 33%

commit v1 on v0

--- a/solution.py
+++ b/solution.py
@@ -12,9 +12,9 @@
 CORES = 2
 VMEM_LIMIT = 16 << 20
 STACKED_HEADS = 4
-UNIT_PARTS = 3
+UNIT_PARTS = 2
 BF16_ROWS = 16
-COLUMNS = 6 * LANES
+COLUMNS = 12 * LANES
 
 masked_value = -1e30
 NT = (((1,), (1,)), ((), ()))

time: 135 us -> 135 us (level)
  no operation moved by 1% of the time
where the time goes in v1:
time: 135 us; the launch traced here: 134 us
  Pallas kernels  59.3 us (44%)
  starting transfers between devices  41.1 us (30%)
  waiting for transfers between devices  28.6 us (21%)
  local copies, waits for them, and re-layouts  4.2 us (3%)
    pallas_call x4, Pallas kernels, expert_rows(): pl.pallas_call(functools.partial(expert_kernel, experts, n_head), out_sha...  34.3 us
    ppermute x9, waiting for transfers between devices, next_chip(): return lax.ppermute(x, 'ctx', to_next_chip)  19.4 us
    ppermute x9, starting transfers between devices, next_chip(): return lax.ppermute(x, 'ctx', to_next_chip)  13.9 us
    ppermute x9, starting transfers between devices, next_head(): lax.ppermute(x, 'head', [(i, (i + j) % n_head) for i in range(n_head)])  12.9 us
    pallas_call x1, Pallas kernels, attend(): pl.pallas_call(functools.partial(attend_kernel, len(kv), n_head), out_sha...  12.7 us
    ppermute x3, starting transfers between devices, body(): lax.ppermute(own, 'ctx', [(i, i + CORES * k) for i in range(n_ctx - CORES...  10.7 us
    pallas_call x1, Pallas kernels, load(): pl.pallas_call(functools.partial(load_kernel, n), out_shape=[pltpu.VMEM(a...  8.33 us
    ppermute x9, waiting for transfers between devices, next_head(): lax.ppermute(x, 'head', [(i, (i + j) % n_head) for i in range(n_head)])  7.16 us
  transfers between devices with their start and end apart: 37, of which 15 were waited for; matrix products, arithmetic and copies ran while one was open for 2% of the time, Pallas kernels for 33%

profile of v1, /device:TPU:0, one launch (start us, length us, event | category | flops | bytes accessed | tf_op | source)
XLA Modules:
  0.0 134.5 jit_solution(17829565407560606535)
XLA Ops:
  0.0 1.0 side_by_side.1.rest_0_
  1.0 7.0 %collective-permute-start.2 = (bf16[128,512]{1,0:T(8,128)(2,1)S(1)}, bf16[128,512]{1,0:T(8,128)(2,1)S(1)}, u32[]{:S(2)}, u32[]{:S(2)}) collective-permute-start(bf16[128,512]{1,0:T(8,128)(2,1)S(1)} %side_by_side.1.rest_0_), channel_id=1, source_target_pairs={{0,12},{2,14},{1,13},{3,15},{16,28},{18,30},{17,29},{19,31}} | collective-permute-start | bytes 393224 | tf_op jit(solution)/shard_map/keys_and_values/ppermute | solution.py:439
  7.9 1.3 collective-permute-start.1
  9.2 2.5 %collective-permute-start = (bf16[128,512]{1,0:T(8,128)(2,1)S(1)}, bf16[128,512]{1,0:T(8,128)(2,1)S(1)}, u32[]{:S(2)}, u32[]{:S(2)}) collective-permute-start(bf16[128,512]{1,0:T(8,128)(2,1)S(1)} %side_by_side.1.rest_0_), channel_id=1, source_target_pairs={{0,4},{2,6},{4,8},{6,10},{8,12},{10,14},{1,5},{3,7},{5,9},{7,11},{... | collective-permute-start | bytes 393224 | tf_op jit(solution)/shard_map/keys_and_values/ppermute | solution.py:439
  11.7 0.8 dynamic-slice_bitcast_fusion
  12.7 1.0 copy-done.2
  13.7 0.7 copy-done.3
  14.4 1.2 prepare.1
  15.6 0.7 collective-permute-done.rest_2_
  16.3 0.5 collective-permute-start.4
  16.8 0.5 collective-permute-start.6
  18.4 12.7 %attend.1 = (bf16[64,2944]{1,0:T(8,128)(2,1)S(1)}, bf16[64,2944]{1,0:T(8,128)(2,1)S(1)}) custom-call(s32[2]{0:T(128)S(1)} %pad_add_fusion.place, f32[32]{0:T(128)S(1)} %copy-done.4, bf16[4096,64]{1,0:T(8,128)(2,1)S(1)} %get-tuple-element.71.q_ref, f32[128,1024]{1,0:T(8,128)S(1)} %get-tuple-element.72.bias, bf16[2880,2048]{1,0:T(8,128)(2,1)} %bitcast.13, ...), custom_call_target="tpu_custom_call" | custom-call | flops 2583691264 | bytes 11796480 | tf_op jit(solution)/shard_map/attention/attend/pallas_call | solution.py:201
  31.2 1.6 %collective-permute-start.7 = (bf16[64,2944]{1,0:T(8,128)(2,1)S(1)}, bf16[64,2944]{1,0:T(8,128)(2,1)S(1)}, u32[]{:S(2)}, u32[]{:S(2)}) collective-permute-start(bf16[64,2944]{1,0:T(8,128)(2,1)S(1)} %get-tuple-element.80), channel_id=1, source_target_pairs={{0,1},{1,0},{2,3},{3,2},{4,5},{5,4},{6,7},{7,6},{8,9},{9,8},{10,11... | collective-permute-start | bytes 1130504 | tf_op jit(solution)/shard_map/norm/ppermute | solution.py:413
  33.3 8.3 %load.1 = (bf16[1440,2880]{1,0:T(8,128)(2,1)S(1)}, bf16[2,1440,2880]{2,1,0:T(8,128)(2,1)S(1)}, f32[8,128]{1,0:T(8,128)S(1)}) custom-call(bf16[1440,2880]{1,0:T(8,128)(2,1)} %bitcast.14, bf16[2,1440,2880]{2,1,0:T(8,128)(2,1)} %bitcast.12, bf16[64,2944]{1,0:T(8,128)(2,1)S(1)} %get-tuple-element.82.refs_2_.refs_0_), custom_call_target="tpu_custom_call" | custom-call | bytes 49766400 | tf_op jit(solution)/shard_map/norm/load/pallas_call | solution.py:40
  41.7 0.6 collective-permute-done.7.refs_1_
  42.2 0.8 norm_and_gates.1
  43.0 4.5 %collective-permute-start.9 = (bf16[64,2944]{1,0:T(8,128)(2,1)S(1)}, bf16[64,2944]{1,0:T(8,128)(2,1)S(1)}, u32[]{:S(2)}, u32[]{:S(2)}) collective-permute-start(bf16[64,2944]{1,0:T(8,128)(2,1)S(1)} %get-tuple-element.87.refs_0_), channel_id=1, source_target_pairs={{0,4},{2,6},{4,12},{6,14},{8,0},{10,2},{12,8},{14,10},{1,5},{3,7},... | collective-permute-start | bytes 1130504 | tf_op jit(solution)/shard_map/rows_of_chips/ppermute | solution.py:410
  47.4 1.5 %collective-permute-start.8 = (bf16[64,2944]{1,0:T(8,128)(2,1)S(1)}, bf16[64,2944]{1,0:T(8,128)(2,1)S(1)}, u32[]{:S(2)}, u32[]{:S(2)}) collective-permute-start(bf16[64,2944]{1,0:T(8,128)(2,1)S(1)} %get-tuple-element.87.refs_0_), channel_id=1, source_target_pairs={{0,1},{1,0},{2,3},{3,2},{4,5},{5,4},{6,7},{7,6},{8,9},{9,8},{10,11... | collective-permute-start | bytes 1130504 | tf_op jit(solution)/shard_map/rows_of_chips/ppermute | solution.py:413
  48.9 8.9 %collective-permute-done.9.refs_0_ = bf16[64,2944]{1,0:T(8,128)(2,1)S(1)} collective-permute-done((bf16[64,2944]{1,0:T(8,128)(2,1)S(1)}, bf16[64,2944]{1,0:T(8,128)(2,1)S(1)}, u32[]{:S(2)}, u32[]{:S(2)}) %collective-permute-start.9) | collective-permute-done | bytes 376864 | tf_op jit(solution)/shard_map/rows_of_chips/ppermute | solution.py:410
  57.8 0.5 collective-permute-start.11
  58.5 1.5 %collective-permute-start.12 = (bf16[64,2944]{1,0:T(8,128)(2,1)S(1)}, bf16[64,2944]{1,0:T(8,128)(2,1)S(1)}, u32[]{:S(2)}, u32[]{:S(2)}) collective-permute-start(bf16[64,2944]{1,0:T(8,128)(2,1)S(1)} %collective-permute-done.9.refs_0_), channel_id=1, source_target_pairs={{0,1},{1,0},{2,3},{3,2},{4,5},{5,4},{6,7},{7,6},{8,9},{9,8},{10,11... | collective-permute-start | bytes 1130504 | tf_op jit(solution)/shard_map/rows_of_chips/ppermute | solution.py:413
  60.0 8.6 %expert_rows.4 = (bf16[64,2944]{1,0:T(8,128)(2,1)S(1)}, bf16[64,2944]{1,0:T(8,128)(2,1)S(1)}, bf16[128,2944]{1,0:T(8,128)(2,1)S(1)}, f32[8,128]{1,0:T(8,128)S(1)}) custom-call(s32[2]{0:T(128)S(1)} %pad_add_fusion.place, bf16[2,1440,2880]{2,1,0:T(8,128)(2,1)S(1)} %get-tuple-element.78.gate_up, bf16[1440,2880]{1,0:T(8,128)(2,1)S(1)} %get-tuple-element.79.down, ...), custom_call_target="tpu_custom_call" | custom-call | flops 6370099200 | bytes 24883200 | tf_op jit(solution)/shard_map/experts/expert_rows/pallas_call | solution.py:323
  68.6 1.3 collective-permute-done.13.refs_0_
  69.9 0.5 collective-permute-start.15
  70.4 2.3 %collective-permute-start.17 = (bf16[64,2944]{1,0:T(8,128)(2,1)S(1)}, bf16[64,2944]{1,0:T(8,128)(2,1)S(1)}, u32[]{:S(2)}, u32[]{:S(2)}) collective-permute-start(bf16[64,2944]{1,0:T(8,128)(2,1)S(1)} %collective-permute-done.13.refs_0_), channel_id=1, source_target_pairs={{0,4},{2,6},{4,12},{6,14},{8,0},{10,2},{12,8},{14,10},{1,5},{3,7},... | collective-permute-start | bytes 1130504 | tf_op jit(solution)/shard_map/rows_of_chips/ppermute | solution.py:410
  72.7 1.5 %collective-permute-start.16 = (bf16[64,2944]{1,0:T(8,128)(2,1)S(1)}, bf16[64,2944]{1,0:T(8,128)(2,1)S(1)}, u32[]{:S(2)}, u32[]{:S(2)}) collective-permute-start(bf16[64,2944]{1,0:T(8,128)(2,1)S(1)} %collective-permute-done.13.refs_0_), channel_id=1, source_target_pairs={{0,1},{1,0},{2,3},{3,2},{4,5},{5,4},{6,7},{7,6},{8,9},{9,8},{10,11... | collective-permute-start | bytes 1130504 | tf_op jit(solution)/shard_map/rows_of_chips/ppermute | solution.py:413
  74.2 8.6 %expert_rows.5 = (bf16[64,2944]{1,0:T(8,128)(2,1)S(1)}, bf16[64,2944]{1,0:T(8,128)(2,1)S(1)}, bf16[128,2944]{1,0:T(8,128)(2,1)S(1)}, f32[8,128]{1,0:T(8,128)S(1)}) custom-call(s32[2]{0:T(128)S(1)} %pad_add_fusion.place, bf16[2,1440,2880]{2,1,0:T(8,128)(2,1)S(1)} %get-tuple-element.78.gate_up, bf16[1440,2880]{1,0:T(8,128)(2,1)S(1)} %get-tuple-element.79.down, ...), custom_call_target="tpu_custom_call" | custom-call | flops 6370099200 | bytes 24883200 | tf_op jit(solution)/shard_map/experts/expert_rows/pallas_call | solution.py:323
  83.1 0.5 collective-permute-start.30
  83.6 1.2 collective-permute-start.21
  84.8 0.5 collective-permute-start.19
  85.4 1.6 %collective-permute-start.22 = (bf16[64,2944]{1,0:T(8,128)(2,1)S(1)}, bf16[64,2944]{1,0:T(8,128)(2,1)S(1)}, u32[]{:S(2)}, u32[]{:S(2)}) collective-permute-start(bf16[64,2944]{1,0:T(8,128)(2,1)S(1)} %add_convert_fusion.3), channel_id=1, source_target_pairs={{0,1},{1,0},{2,3},{3,2},{4,5},{5,4},{6,7},{7,6},{8,9},{9,8},{10,11... | collective-permute-start | bytes 1130504 | tf_op jit(solution)/shard_map/sum_back/ppermute | solution.py:413
  87.5 8.6 %expert_rows.6 = (bf16[64,2944]{1,0:T(8,128)(2,1)S(1)}, bf16[64,2944]{1,0:T(8,128)(2,1)S(1)}, bf16[128,2944]{1,0:T(8,128)(2,1)S(1)}, f32[8,128]{1,0:T(8,128)S(1)}) custom-call(s32[2]{0:T(128)S(1)} %pad_add_fusion.place, bf16[2,1440,2880]{2,1,0:T(8,128)(2,1)S(1)} %get-tuple-element.78.gate_up, bf16[1440,2880]{1,0:T(8,128)(2,1)S(1)} %get-tuple-element.79.down, ...), custom_call_target="tpu_custom_call" | custom-call | flops 6370099200 | bytes 24883200 | tf_op jit(solution)/shard_map/experts/expert_rows/pallas_call | solution.py:323
  96.4 0.7 slice-done
  97.2 1.2 collective-permute-start.27
  98.5 0.5 collective-permute-start.25
  99.1 1.6 %collective-permute-start.26 = (bf16[64,2944]{1,0:T(8,128)(2,1)S(1)}, bf16[64,2944]{1,0:T(8,128)(2,1)S(1)}, u32[]{:S(2)}, u32[]{:S(2)}) collective-permute-start(bf16[64,2944]{1,0:T(8,128)(2,1)S(1)} %add_convert_fusion.2), channel_id=1, source_target_pairs={{0,1},{1,0},{2,3},{3,2},{4,5},{5,4},{6,7},{7,6},{8,9},{9,8},{10,11... | collective-permute-start | bytes 1130504 | tf_op jit(solution)/shard_map/sum_back/ppermute | solution.py:413
  100.7 8.6 %expert_rows.7 = (bf16[64,2944]{1,0:T(8,128)(2,1)S(1)}, bf16[64,2944]{1,0:T(8,128)(2,1)S(1)}, bf16[128,2944]{1,0:T(8,128)(2,1)S(1)}, f32[8,128]{1,0:T(8,128)S(1)}) custom-call(s32[2]{0:T(128)S(1)} %pad_add_fusion.place, bf16[2,1440,2880]{2,1,0:T(8,128)(2,1)S(1)} %get-tuple-element.78.gate_up, bf16[1440,2880]{1,0:T(8,128)(2,1)S(1)} %get-tuple-element.79.down, ...), custom_call_target="tpu_custom_call" | custom-call | flops 6370099200 | bytes 24883200 | tf_op jit(solution)/shard_map/experts/expert_rows/pallas_call | solution.py:323
  109.3 0.5 collective-permute-done.26
  109.9 1.2 collective-permute-start.35
  111.3 1.0 collective-permute-start.32
  112.3 1.6 %collective-permute-start.29 = (bf16[64,1536]{1,0:T(8,128)(2,1)S(1)}, bf16[64,1536]{1,0:T(8,128)(2,1)S(1)}, u32[]{:S(2)}, u32[]{:S(2)}) collective-permute-start(bf16[64,1536]{1,0:T(8,128)(2,1)S(1)} %add_convert_fusion.6), channel_id=1, source_target_pairs={{0,1},{1,0},{2,3},{3,2},{4,5},{5,4},{6,7},{7,6},{8,9},{9,8},{10,11... | collective-permute-start | bytes 589832 | tf_op jit(solution)/shard_map/sum_back/ppermute | solution.py:413
  113.9 0.6 collective-permute-start.34
  114.5 5.6 %collective-permute-done.29 = bf16[64,1536]{1,0:T(8,128)(2,1)S(1)} collective-permute-done((bf16[64,1536]{1,0:T(8,128)(2,1)S(1)}, bf16[64,1536]{1,0:T(8,128)(2,1)S(1)}, u32[]{:S(2)}, u32[]{:S(2)}) %collective-permute-start.29) | collective-permute-done | bytes 196640 | tf_op jit(solution)/shard_map/sum_back/ppermute | solution.py:413
  120.1 1.9 %collective-permute-done.32 = bf16[64,1536]{1,0:T(8,128)(2,1)S(1)} collective-permute-done((bf16[64,1536]{1,0:T(8,128)(2,1)S(1)}, bf16[64,1536]{1,0:T(8,128)(2,1)S(1)}, u32[]{:S(2)}, u32[]{:S(2)}) %collective-permute-start.32) | collective-permute-done | bytes 196640 | tf_op jit(solution)/shard_map/sum_back/ppermute | solution.py:410
  122.6 1.6 %collective-permute-start.31 = (bf16[64,2944]{1,0:T(8,128)(2,1)S(1)}, bf16[64,2944]{1,0:T(8,128)(2,1)S(1)}, u32[]{:S(2)}, u32[]{:S(2)}) collective-permute-start(bf16[64,2944]{1,0:T(8,128)(2,1)S(1)} %add_convert_fusion), channel_id=1, source_target_pairs={{0,1},{1,0},{2,3},{3,2},{4,5},{5,4},{6,7},{7,6},{8,9},{9,8},{10,11... | collective-permute-start | bytes 1130504 | tf_op jit(solution)/shard_map/sum_back/ppermute | solution.py:413
  124.3 1.9 %collective-permute-start.36 = (bf16[64,1408]{1,0:T(8,128)(2,1)S(1)}, bf16[64,1408]{1,0:T(8,128)(2,1)S(1)}, u32[]{:S(2)}, u32[]{:S(2)}) collective-permute-start(bf16[64,1408]{1,0:T(8,128)(2,1)S(1)} %add_convert_fusion.7), channel_id=1, source_target_pairs={{0,4},{2,6},{4,12},{6,14},{8,0},{10,2},{12,8},{14,10},{1,5},{3,7},... | collective-permute-start | bytes 540680 | tf_op jit(solution)/shard_map/sum_back/ppermute | solution.py:410
  126.2 7.3 %collective-permute-done.36.refs_5_ = bf16[64,1408]{1,0:T(8,128)(2,1)S(1)} collective-permute-done((bf16[64,1408]{1,0:T(8,128)(2,1)S(1)}, bf16[64,1408]{1,0:T(8,128)(2,1)S(1)}, u32[]{:S(2)}, u32[]{:S(2)}) %collective-permute-start.36) | collective-permute-done | bytes 180256 | tf_op jit(solution)/shard_map/sum_back/ppermute | solution.py:410
  133.5 1.0 finish.1
  (78 shorter events, 4.4 us)
Async XLA Ops:
  0.0 17.4 %copy-start = (bf16[128,2880]{0,1:T(8,128)(2,1)S(1)}, bf16[128,2880]{0,1:T(8,128)(2,1)}, u32[]{:S(2)}) copy-start(bf16[128,2880]{0,1:T(8,128)(2,1)} %param.17) | copy-start | bytes 2211844
  0.0 18.4 %copy-start.4 = (f32[32]{0:T(128)S(1)}, f32[32]{0:T(128)}, u32[]{:S(2)}) copy-start(f32[32]{0:T(128)} %sinks.1) | copy-start | bytes 388
  1.0 14.6 %collective-permute-start.2 = (bf16[128,512]{1,0:T(8,128)(2,1)S(1)}, bf16[128,512]{1,0:T(8,128)(2,1)S(1)}, u32[]{:S(2)}, u32[]{:S(2)}) collective-permute-start(bf16[128,512]{1,0:T(8,128)(2,1)S(1)} %side_by_side.1.rest_0_), channel_id=1, source_target_pairs={{0,12},{2,14},{1,13},{3,15},{16,28},{18,30},{17,29},{19,31}} | collective-permute-start | bytes 393224 | tf_op jit(solution)/shard_map/keys_and_values/ppermute | solution.py:439
  7.9 7.7 %collective-permute-start.1 = (bf16[128,512]{1,0:T(8,128)(2,1)S(1)}, bf16[128,512]{1,0:T(8,128)(2,1)S(1)}, u32[]{:S(2)}, u32[]{:S(2)}) collective-permute-start(bf16[128,512]{1,0:T(8,128)(2,1)S(1)} %side_by_side.1.rest_0_), channel_id=1, source_target_pairs={{0,8},{2,10},{4,12},{6,14},{1,9},{3,11},{5,13},{7,15},{16,24},{18,... | collective-permute-start | bytes 393224 | tf_op jit(solution)/shard_map/keys_and_values/ppermute | solution.py:439
  9.2 7.1 %collective-permute-start = (bf16[128,512]{1,0:T(8,128)(2,1)S(1)}, bf16[128,512]{1,0:T(8,128)(2,1)S(1)}, u32[]{:S(2)}, u32[]{:S(2)}) collective-permute-start(bf16[128,512]{1,0:T(8,128)(2,1)S(1)} %side_by_side.1.rest_0_), channel_id=1, source_target_pairs={{0,4},{2,6},{4,8},{6,10},{8,12},{10,14},{1,5},{3,7},{5,9},{7,11},{... | collective-permute-start | bytes 393224 | tf_op jit(solution)/shard_map/keys_and_values/ppermute | solution.py:439
  12.7 1.0 copy-start.2
  13.7 0.7 copy-start.3
  16.3 1.3 %collective-permute-start.3 = (bf16[128,512]{1,0:T(8,128)(2,1)S(1)}, bf16[128,512]{1,0:T(8,128)(2,1)S(1)}, u32[]{:S(2)}, u32[]{:S(2)}) collective-permute-start(bf16[128,512]{1,0:T(8,128)(2,1)S(1)} %side_by_side.1.rest_0_), channel_id=1, source_target_pairs={{0,2},{2,0},{4,6},{6,4},{8,10},{10,8},{12,14},{14,12},{1,3},{3,1},... | collective-permute-start | bytes 393224 | tf_op jit(solution)/shard_map/attention/ppermute | solution.py:407
  16.3 1.5 %collective-permute-start.4 = (bf16[128,512]{1,0:T(8,128)(2,1)S(1)}, bf16[128,512]{1,0:T(8,128)(2,1)S(1)}, u32[]{:S(2)}, u32[]{:S(2)}) collective-permute-start(bf16[128,512]{1,0:T(8,128)(2,1)S(1)} %collective-permute-done.rest_2_), channel_id=1, source_target_pairs={{0,2},{2,0},{4,6},{6,4},{8,10},{10,8},{12,14},{14,12},{1,3},{3,1},... | collective-permute-start | bytes 393224 | tf_op jit(solution)/shard_map/attention/ppermute | solution.py:407
  16.8 1.3 %collective-permute-start.5 = (bf16[128,512]{1,0:T(8,128)(2,1)S(1)}, bf16[128,512]{1,0:T(8,128)(2,1)S(1)}, u32[]{:S(2)}, u32[]{:S(2)}) collective-permute-start(bf16[128,512]{1,0:T(8,128)(2,1)S(1)} %collective-permute-done.1.rest_4_), channel_id=1, source_target_pairs={{0,2},{2,0},{4,6},{6,4},{8,10},{10,8},{12,14},{14,12},{1,3},{3,1},... | collective-permute-start | bytes 393224 | tf_op jit(solution)/shard_map/attention/ppermute | solution.py:407
  16.8 1.5 %collective-permute-start.6 = (bf16[128,512]{1,0:T(8,128)(2,1)S(1)}, bf16[128,512]{1,0:T(8,128)(2,1)S(1)}, u32[]{:S(2)}, u32[]{:S(2)}) collective-permute-start(bf16[128,512]{1,0:T(8,128)(2,1)S(1)} %collective-permute-done.2.rest_6_), channel_id=1, source_target_pairs={{0,2},{2,0},{4,6},{6,4},{8,10},{10,8},{12,14},{14,12},{1,3},{3,1},... | collective-permute-start | bytes 393224 | tf_op jit(solution)/shard_map/attention/ppermute | solution.py:407
  18.4 14.3 %copy-start.8 = (s32[128,4]{0,1:T(4,128)S(1)}, s32[128,4]{0,1:T(4,128)}, u32[]{:S(2)}) copy-start(s32[128,4]{0,1:T(4,128)} %param.18) | copy-start | bytes 6148
  18.4 14.4 %copy-start.7 = (f32[2880]{0:T(1024)S(1)}, f32[2880]{0:T(1024)}, u32[]{:S(2)}) copy-start(f32[2880]{0:T(1024)} %param.20) | copy-start | bytes 34564
  31.1 2.1 %copy-start.6 = (bf16[2880,8]{0,1:T(8,128)(2,1)S(1)}, bf16[2880,8]{0,1:T(8,128)(2,1)}, u32[]{:S(2)}) copy-start(bf16[2880,8]{0,1:T(8,128)(2,1)} %param.21) | copy-start | bytes 138244
  31.2 11.1 %collective-permute-start.7 = (bf16[64,2944]{1,0:T(8,128)(2,1)S(1)}, bf16[64,2944]{1,0:T(8,128)(2,1)S(1)}, u32[]{:S(2)}, u32[]{:S(2)}) collective-permute-start(bf16[64,2944]{1,0:T(8,128)(2,1)S(1)} %get-tuple-element.80), channel_id=1, source_target_pairs={{0,1},{1,0},{2,3},{3,2},{4,5},{5,4},{6,7},{7,6},{8,9},{9,8},{10,11... | collective-permute-start | bytes 1130504 | tf_op jit(solution)/shard_map/norm/ppermute | solution.py:413
  43.0 14.8 %collective-permute-start.9 = (bf16[64,2944]{1,0:T(8,128)(2,1)S(1)}, bf16[64,2944]{1,0:T(8,128)(2,1)S(1)}, u32[]{:S(2)}, u32[]{:S(2)}) collective-permute-start(bf16[64,2944]{1,0:T(8,128)(2,1)S(1)} %get-tuple-element.87.refs_0_), channel_id=1, source_target_pairs={{0,4},{2,6},{4,12},{6,14},{8,0},{10,2},{12,8},{14,10},{1,5},{3,7},... | collective-permute-start | bytes 1130504 | tf_op jit(solution)/shard_map/rows_of_chips/ppermute | solution.py:410
  47.4 10.4 %collective-permute-start.8 = (bf16[64,2944]{1,0:T(8,128)(2,1)S(1)}, bf16[64,2944]{1,0:T(8,128)(2,1)S(1)}, u32[]{:S(2)}, u32[]{:S(2)}) collective-permute-start(bf16[64,2944]{1,0:T(8,128)(2,1)S(1)} %get-tuple-element.87.refs_0_), channel_id=1, source_target_pairs={{0,1},{1,0},{2,3},{3,2},{4,5},{5,4},{6,7},{7,6},{8,9},{9,8},{10,11... | collective-permute-start | bytes 1130504 | tf_op jit(solution)/shard_map/rows_of_chips/ppermute | solution.py:413
  57.8 2.2 %collective-permute-start.10 = (bf16[64,2944]{1,0:T(8,128)(2,1)S(1)}, bf16[64,2944]{1,0:T(8,128)(2,1)S(1)}, u32[]{:S(2)}, u32[]{:S(2)}) collective-permute-start(bf16[64,2944]{1,0:T(8,128)(2,1)S(1)} %get-tuple-element.87.refs_0_), channel_id=1, source_target_pairs={{0,2},{2,0},{4,6},{6,4},{8,10},{10,8},{12,14},{14,12},{1,3},{3,1},... | collective-permute-start | bytes 1130504 | tf_op jit(solution)/shard_map/experts/ppermute | solution.py:407
  57.8 2.2 %collective-permute-start.11 = (bf16[64,2944]{1,0:T(8,128)(2,1)S(1)}, bf16[64,2944]{1,0:T(8,128)(2,1)S(1)}, u32[]{:S(2)}, u32[]{:S(2)}) collective-permute-start(bf16[64,2944]{1,0:T(8,128)(2,1)S(1)} %collective-permute-done.8.refs_1_), channel_id=1, source_target_pairs={{0,2},{2,0},{4,6},{6,4},{8,10},{10,8},{12,14},{14,12},{1,3},{3,1},... | collective-permute-start | bytes 1130504 | tf_op jit(solution)/shard_map/experts/ppermute | solution.py:407
  58.3 11.6 %collective-permute-start.13 = (bf16[64,2944]{1,0:T(8,128)(2,1)S(1)}, bf16[64,2944]{1,0:T(8,128)(2,1)S(1)}, u32[]{:S(2)}, u32[]{:S(2)}) collective-permute-start(bf16[64,2944]{1,0:T(8,128)(2,1)S(1)} %collective-permute-done.9.refs_0_), channel_id=1, source_target_pairs={{0,4},{2,6},{4,12},{6,14},{8,0},{10,2},{12,8},{14,10},{1,5},{3,7},... | collective-permute-start | bytes 1130504 | tf_op jit(solution)/shard_map/rows_of_chips/ppermute | solution.py:410
  58.5 11.4 %collective-permute-start.12 = (bf16[64,2944]{1,0:T(8,128)(2,1)S(1)}, bf16[64,2944]{1,0:T(8,128)(2,1)S(1)}, u32[]{:S(2)}, u32[]{:S(2)}) collective-permute-start(bf16[64,2944]{1,0:T(8,128)(2,1)S(1)} %collective-permute-done.9.refs_0_), channel_id=1, source_target_pairs={{0,1},{1,0},{2,3},{3,2},{4,5},{5,4},{6,7},{7,6},{8,9},{9,8},{10,11... | collective-permute-start | bytes 1130504 | tf_op jit(solution)/shard_map/rows_of_chips/ppermute | solution.py:413
  69.9 4.3 %collective-permute-start.14 = (bf16[64,2944]{1,0:T(8,128)(2,1)S(1)}, bf16[64,2944]{1,0:T(8,128)(2,1)S(1)}, u32[]{:S(2)}, u32[]{:S(2)}) collective-permute-start(bf16[64,2944]{1,0:T(8,128)(2,1)S(1)} %collective-permute-done.9.refs_0_), channel_id=1, source_target_pairs={{0,2},{2,0},{4,6},{6,4},{8,10},{10,8},{12,14},{14,12},{1,3},{3,1},... | collective-permute-start | bytes 1130504 | tf_op jit(solution)/shard_map/experts/ppermute | solution.py:407
  69.9 4.3 %collective-permute-start.15 = (bf16[64,2944]{1,0:T(8,128)(2,1)S(1)}, bf16[64,2944]{1,0:T(8,128)(2,1)S(1)}, u32[]{:S(2)}, u32[]{:S(2)}) collective-permute-start(bf16[64,2944]{1,0:T(8,128)(2,1)S(1)} %collective-permute-done.12.refs_1_), channel_id=1, source_target_pairs={{0,2},{2,0},{4,6},{6,4},{8,10},{10,8},{12,14},{14,12},{1,3},{3,1},... | collective-permute-start | bytes 1130504 | tf_op jit(solution)/shard_map/experts/ppermute | solution.py:407
  70.4 12.4 %collective-permute-start.17 = (bf16[64,2944]{1,0:T(8,128)(2,1)S(1)}, bf16[64,2944]{1,0:T(8,128)(2,1)S(1)}, u32[]{:S(2)}, u32[]{:S(2)}) collective-permute-start(bf16[64,2944]{1,0:T(8,128)(2,1)S(1)} %collective-permute-done.13.refs_0_), channel_id=1, source_target_pairs={{0,4},{2,6},{4,12},{6,14},{8,0},{10,2},{12,8},{14,10},{1,5},{3,7},... | collective-permute-start | bytes 1130504 | tf_op jit(solution)/shard_map/rows_of_chips/ppermute | solution.py:410
  72.7 10.4 %collective-permute-start.16 = (bf16[64,2944]{1,0:T(8,128)(2,1)S(1)}, bf16[64,2944]{1,0:T(8,128)(2,1)S(1)}, u32[]{:S(2)}, u32[]{:S(2)}) collective-permute-start(bf16[64,2944]{1,0:T(8,128)(2,1)S(1)} %collective-permute-done.13.refs_0_), channel_id=1, source_target_pairs={{0,1},{1,0},{2,3},{3,2},{4,5},{5,4},{6,7},{7,6},{8,9},{9,8},{10,11... | collective-permute-start | bytes 1130504 | tf_op jit(solution)/shard_map/rows_of_chips/ppermute | solution.py:413
  83.1 2.2 %collective-permute-start.18 = (bf16[128,2944]{1,0:T(8,128)(2,1)S(1)}, bf16[128,2944]{1,0:T(8,128)(2,1)S(1)}, u32[]{:S(2)}, u32[]{:S(2)}) collective-permute-start(bf16[128,2944]{1,0:T(8,128)(2,1)S(1)} %get-tuple-element.97), channel_id=1, source_target_pairs={{0,2},{2,0},{4,6},{6,4},{8,10},{10,8},{12,14},{14,12},{1,3},{3,1},... | collective-permute-start | bytes 2261000 | tf_op jit(solution)/shard_map/sum_back/ppermute | solution.py:407
  83.1 13.2 %collective-permute-start.30 = (bf16[128,2944]{1,0:T(8,128)(2,1)S(1)}, bf16[128,2944]{1,0:T(8,128)(2,1)S(1)}, u32[]{:S(2)}, u32[]{:S(2)}) collective-permute-start(bf16[128,2944]{1,0:T(8,128)(2,1)S(1)} %get-tuple-element.122), channel_id=1, source_target_pairs={{0,2},{2,0},{4,6},{6,4},{8,10},{10,8},{12,14},{14,12},{1,3},{3,1},... | collective-permute-start | bytes 2261000 | tf_op jit(solution)/shard_map/sum_back/ppermute | solution.py:407
  83.6 12.5 %collective-permute-start.21 = (bf16[64,2944]{1,0:T(8,128)(2,1)S(1)}, bf16[64,2944]{1,0:T(8,128)(2,1)S(1)}, u32[]{:S(2)}, u32[]{:S(2)}) collective-permute-start(bf16[64,2944]{1,0:T(8,128)(2,1)S(1)} %collective-permute-done.16.refs_1_), channel_id=1, source_target_pairs={{0,4},{2,6},{4,12},{6,14},{8,0},{10,2},{12,8},{14,10},{1,5},{3,7},... | collective-permute-start | bytes 1130504 | tf_op jit(solution)/shard_map/rows_of_chips/ppermute | solution.py:410
  84.8 2.7 %collective-permute-start.20 = (bf16[64,2944]{1,0:T(8,128)(2,1)S(1)}, bf16[64,2944]{1,0:T(8,128)(2,1)S(1)}, u32[]{:S(2)}, u32[]{:S(2)}) collective-permute-start(bf16[64,2944]{1,0:T(8,128)(2,1)S(1)} %collective-permute-done.16.refs_1_), channel_id=1, source_target_pairs={{0,2},{2,0},{4,6},{6,4},{8,10},{10,8},{12,14},{14,12},{1,3},{3,1},... | collective-permute-start | bytes 1130504 | tf_op jit(solution)/shard_map/experts/ppermute | solution.py:407
  84.8 2.7 %collective-permute-start.19 = (bf16[64,2944]{1,0:T(8,128)(2,1)S(1)}, bf16[64,2944]{1,0:T(8,128)(2,1)S(1)}, u32[]{:S(2)}, u32[]{:S(2)}) collective-permute-start(bf16[64,2944]{1,0:T(8,128)(2,1)S(1)} %collective-permute-done.13.refs_0_), channel_id=1, source_target_pairs={{0,2},{2,0},{4,6},{6,4},{8,10},{10,8},{12,14},{14,12},{1,3},{3,1},... | collective-permute-start | bytes 1130504 | tf_op jit(solution)/shard_map/experts/ppermute | solution.py:407
  85.3 10.8 %copy-start.5 = (bf16[128,2944]{1,0:T(8,128)(2,1)}, bf16[128,2944]{1,0:T(8,128)(2,1)S(1)}, u32[]{:S(2)}) copy-start(bf16[128,2944]{1,0:T(8,128)(2,1)S(1)} %collective-permute-done.18) | copy-start | bytes 2260996
  85.4 10.9 %collective-permute-start.22 = (bf16[64,2944]{1,0:T(8,128)(2,1)S(1)}, bf16[64,2944]{1,0:T(8,128)(2,1)S(1)}, u32[]{:S(2)}, u32[]{:S(2)}) collective-permute-start(bf16[64,2944]{1,0:T(8,128)(2,1)S(1)} %add_convert_fusion.3), channel_id=1, source_target_pairs={{0,1},{1,0},{2,3},{3,2},{4,5},{5,4},{6,7},{7,6},{8,9},{9,8},{10,11... | collective-permute-start | bytes 1130504 | tf_op jit(solution)/shard_map/sum_back/ppermute | solution.py:413
  96.1 1.0 slice-start
  96.3 2.7 %collective-permute-start.23 = (bf16[128,2944]{1,0:T(8,128)(2,1)S(1)}, bf16[128,2944]{1,0:T(8,128)(2,1)S(1)}, u32[]{:S(2)}, u32[]{:S(2)}) collective-permute-start(bf16[128,2944]{1,0:T(8,128)(2,1)S(1)} %get-tuple-element.107), channel_id=1, source_target_pairs={{0,2},{2,0},{4,6},{6,4},{8,10},{10,8},{12,14},{14,12},{1,3},{3,1},... | collective-permute-start | bytes 2261000 | tf_op jit(solution)/shard_map/sum_back/ppermute | solution.py:407
  97.2 12.1 %collective-permute-start.27 = (bf16[64,2944]{1,0:T(8,128)(2,1)S(1)}, bf16[64,2944]{1,0:T(8,128)(2,1)S(1)}, u32[]{:S(2)}, u32[]{:S(2)}) collective-permute-start(bf16[64,2944]{1,0:T(8,128)(2,1)S(1)} %add_convert_fusion.1), channel_id=1, source_target_pairs={{0,4},{2,6},{4,12},{6,14},{8,0},{10,2},{12,8},{14,10},{1,5},{3,7},... | collective-permute-start | bytes 1130504 | tf_op jit(solution)/shard_map/sum_back/ppermute | solution.py:410
  98.5 2.2 %collective-permute-start.24 = (bf16[64,2944]{1,0:T(8,128)(2,1)S(1)}, bf16[64,2944]{1,0:T(8,128)(2,1)S(1)}, u32[]{:S(2)}, u32[]{:S(2)}) collective-permute-start(bf16[64,2944]{1,0:T(8,128)(2,1)S(1)} %collective-permute-done.17.refs_0_), channel_id=1, source_target_pairs={{0,2},{2,0},{4,6},{6,4},{8,10},{10,8},{12,14},{14,12},{1,3},{3,1},... | collective-permute-start | bytes 1130504 | tf_op jit(solution)/shard_map/experts/ppermute | solution.py:407
  98.5 2.2 %collective-permute-start.25 = (bf16[64,2944]{1,0:T(8,128)(2,1)S(1)}, bf16[64,2944]{1,0:T(8,128)(2,1)S(1)}, u32[]{:S(2)}, u32[]{:S(2)}) collective-permute-start(bf16[64,2944]{1,0:T(8,128)(2,1)S(1)} %collective-permute-done.21.refs_1_), channel_id=1, source_target_pairs={{0,2},{2,0},{4,6},{6,4},{8,10},{10,8},{12,14},{14,12},{1,3},{3,1},... | collective-permute-start | bytes 1130504 | tf_op jit(solution)/shard_map/experts/ppermute | solution.py:407
  99.1 10.7 %collective-permute-start.26 = (bf16[64,2944]{1,0:T(8,128)(2,1)S(1)}, bf16[64,2944]{1,0:T(8,128)(2,1)S(1)}, u32[]{:S(2)}, u32[]{:S(2)}) collective-permute-start(bf16[64,2944]{1,0:T(8,128)(2,1)S(1)} %add_convert_fusion.2), channel_id=1, source_target_pairs={{0,1},{1,0},{2,3},{3,2},{4,5},{5,4},{6,7},{7,6},{8,9},{9,8},{10,11... | collective-permute-start | bytes 1130504 | tf_op jit(solution)/shard_map/sum_back/ppermute | solution.py:413
  109.8 2.4 %collective-permute-start.28 = (bf16[128,2944]{1,0:T(8,128)(2,1)S(1)}, bf16[128,2944]{1,0:T(8,128)(2,1)S(1)}, u32[]{:S(2)}, u32[]{:S(2)}) collective-permute-start(bf16[128,2944]{1,0:T(8,128)(2,1)S(1)} %get-tuple-element.120), channel_id=1, source_target_pairs={{0,2},{2,0},{4,6},{6,4},{8,10},{10,8},{12,14},{14,12},{1,3},{3,1},... | collective-permute-start | bytes 2261000 | tf_op jit(solution)/shard_map/sum_back/ppermute | solution.py:407
  109.9 14.2 %collective-permute-start.35 = (bf16[64,1408]{1,0:T(8,128)(2,1)S(1)}, bf16[64,1408]{1,0:T(8,128)(2,1)S(1)}, u32[]{:S(2)}, u32[]{:S(2)}) collective-permute-start(bf16[64,1408]{1,0:T(8,128)(2,1)S(1)} %add_convert_fusion.8), channel_id=1, source_target_pairs={{0,4},{2,6},{4,12},{6,14},{8,0},{10,2},{12,8},{14,10},{1,5},{3,7},... | collective-permute-start | bytes 540680 | tf_op jit(solution)/shard_map/sum_back/ppermute | solution.py:410
  111.3 10.8 %collective-permute-start.32 = (bf16[64,1536]{1,0:T(8,128)(2,1)S(1)}, bf16[64,1536]{1,0:T(8,128)(2,1)S(1)}, u32[]{:S(2)}, u32[]{:S(2)}) collective-permute-start(bf16[64,1536]{1,0:T(8,128)(2,1)S(1)} %add_convert_fusion.5), channel_id=1, source_target_pairs={{0,4},{2,6},{4,12},{6,14},{8,0},{10,2},{12,8},{14,10},{1,5},{3,7},... | collective-permute-start | bytes 589832 | tf_op jit(solution)/shard_map/sum_back/ppermute | solution.py:410
  112.3 7.8 %collective-permute-start.29 = (bf16[64,1536]{1,0:T(8,128)(2,1)S(1)}, bf16[64,1536]{1,0:T(8,128)(2,1)S(1)}, u32[]{:S(2)}, u32[]{:S(2)}) collective-permute-start(bf16[64,1536]{1,0:T(8,128)(2,1)S(1)} %add_convert_fusion.6), channel_id=1, source_target_pairs={{0,1},{1,0},{2,3},{3,2},{4,5},{5,4},{6,7},{7,6},{8,9},{9,8},{10,11... | collective-permute-start | bytes 589832 | tf_op jit(solution)/shard_map/sum_back/ppermute | solution.py:413
  113.9 10.2 %collective-permute-start.34 = (bf16[64,1408]{1,0:T(8,128)(2,1)S(1)}, bf16[64,1408]{1,0:T(8,128)(2,1)S(1)}, u32[]{:S(2)}, u32[]{:S(2)}) collective-permute-start(bf16[64,1408]{1,0:T(8,128)(2,1)S(1)} %add_convert_fusion.9), channel_id=1, source_target_pairs={{0,1},{1,0},{2,3},{3,2},{4,5},{5,4},{6,7},{7,6},{8,9},{9,8},{10,11... | collective-permute-start | bytes 540680 | tf_op jit(solution)/shard_map/sum_back/ppermute | solution.py:413
  122.2 11.3 %collective-permute-start.33 = (bf16[64,1536]{1,0:T(8,128)(2,1)S(1)}, bf16[64,1536]{1,0:T(8,128)(2,1)S(1)}, u32[]{:S(2)}, u32[]{:S(2)}) collective-permute-start(bf16[64,1536]{1,0:T(8,128)(2,1)S(1)} %add_convert_fusion.4), channel_id=1, source_target_pairs={{0,4},{2,6},{4,12},{6,14},{8,0},{10,2},{12,8},{14,10},{1,5},{3,7},... | collective-permute-start | bytes 589832 | tf_op jit(solution)/shard_map/sum_back/ppermute | solution.py:410
  122.5 12.0 %copy-start.1 = (bf16[128,2880]{0,1:T(8,128)(2,1)S(1)}, bf16[128,2880]{0,1:T(8,128)(2,1)}, u32[]{:S(2)}) copy-start(bf16[128,2880]{0,1:T(8,128)(2,1)} %param.17) | copy-start | bytes 2211844
  122.6 10.9 %collective-permute-start.31 = (bf16[64,2944]{1,0:T(8,128)(2,1)S(1)}, bf16[64,2944]{1,0:T(8,128)(2,1)S(1)}, u32[]{:S(2)}, u32[]{:S(2)}) collective-permute-start(bf16[64,2944]{1,0:T(8,128)(2,1)S(1)} %add_convert_fusion), channel_id=1, source_target_pairs={{0,1},{1,0},{2,3},{3,2},{4,5},{5,4},{6,7},{7,6},{8,9},{9,8},{10,11... | collective-permute-start | bytes 1130504 | tf_op jit(solution)/shard_map/sum_back/ppermute | solution.py:413
  124.3 9.2 %collective-permute-start.36 = (bf16[64,1408]{1,0:T(8,128)(2,1)S(1)}, bf16[64,1408]{1,0:T(8,128)(2,1)S(1)}, u32[]{:S(2)}, u32[]{:S(2)}) collective-permute-start(bf16[64,1408]{1,0:T(8,128)(2,1)S(1)} %add_convert_fusion.7), channel_id=1, source_target_pairs={{0,4},{2,6},{4,12},{6,14},{8,0},{10,2},{12,8},{14,10},{1,5},{3,7},... | collective-permute-start | bytes 540680 | tf_op jit(solution)/shard_map/sum_back/ppermute | solution.py:410

commit v2 on v1

--- a/solution.py
+++ b/solution.py
@@ -465,7 +465,7 @@
         chunk = next_chip(rows)
         near, chunk, flag = lax.optimization_barrier((near, chunk, flag))
 
-    middle = -(-width // LANES // 2) * LANES
+    middle = -(-width // LANES // 3) * LANES
     halves = [slice(0, middle), slice(middle, width)]
     waiting, arriving = None, []
     for hop in range(n_z):

time: 135 us -> 135 us (level)
  transfers between devices with their start and end apart: 37 -> 37, of which waited for: 15 -> 17; matrix products, arithmetic and copies ran while one was open for 2% -> 2% of each run, Pallas kernels for 33% -> 33%
where the time goes in v2:
time: 135 us
  Pallas kernels  59.3 us (44%)
  starting transfers between devices  41.9 us (31%)
  waiting for transfers between devices  28.8 us (21%)
  local copies, waits for them, and re-layouts  3.51 us (3%)
    pallas_call x4, Pallas kernels, expert_rows(): pl.pallas_call(functools.partial(expert_kernel, experts, n_head), out_sha...  34.3 us
    ppermute x9, waiting for transfers between devices, next_chip(): return lax.ppermute(x, 'ctx', to_next_chip)  18.4 us
    ppermute x9, starting transfers between devices, next_chip(): return lax.ppermute(x, 'ctx', to_next_chip)  14.6 us
    ppermute x9, starting transfers between devices, next_head(): lax.ppermute(x, 'head', [(i, (i + j) % n_head) for i in range(n_head)])  12.9 us
    pallas_call x1, Pallas kernels, attend(): pl.pallas_call(functools.partial(attend_kernel, len(kv), n_head), out_sha...  12.7 us
    ppermute x3, starting transfers between devices, body(): lax.ppermute(own, 'ctx', [(i, i + CORES * k) for i in range(n_ctx - CORES...  10.7 us
    pallas_call x1, Pallas kernels, load(): pl.pallas_call(functools.partial(load_kernel, n), out_shape=[pltpu.VMEM(a...  8.33 us
    ppermute x9, waiting for transfers between devices, next_head(): lax.ppermute(x, 'head', [(i, (i + j) % n_head) for i in range(n_head)])  8.12 us
  transfers between devices with their start and end apart: 37, of which 17 were waited for; matrix products, arithmetic and copies ran while one was open for 2% of the time, Pallas kernels for 33%

profile of v2, /device:TPU:0, one launch (start us, length us, event | category | flops | bytes accessed | tf_op | source)
XLA Modules:
  0.0 134.8 jit_solution(12513978673083264829)
XLA Ops:
  0.0 1.0 side_by_side.1.rest_0_
  1.0 7.0 %collective-permute-start.2 = (bf16[128,512]{1,0:T(8,128)(2,1)S(1)}, bf16[128,512]{1,0:T(8,128)(2,1)S(1)}, u32[]{:S(2)}, u32[]{:S(2)}) collective-permute-start(bf16[128,512]{1,0:T(8,128)(2,1)S(1)} %side_by_side.1.rest_0_), channel_id=1, source_target_pairs={{0,12},{2,14},{1,13},{3,15},{16,28},{18,30},{17,29},{19,31}} | collective-permute-start | bytes 393224 | tf_op jit(solution)/shard_map/keys_and_values/ppermute | solution.py:439
  7.9 1.3 collective-permute-start.1
  9.2 2.5 %collective-permute-start = (bf16[128,512]{1,0:T(8,128)(2,1)S(1)}, bf16[128,512]{1,0:T(8,128)(2,1)S(1)}, u32[]{:S(2)}, u32[]{:S(2)}) collective-permute-start(bf16[128,512]{1,0:T(8,128)(2,1)S(1)} %side_by_side.1.rest_0_), channel_id=1, source_target_pairs={{0,4},{2,6},{4,8},{6,10},{8,12},{10,14},{1,5},{3,7},{5,9},{7,11},{... | collective-permute-start | bytes 393224 | tf_op jit(solution)/shard_map/keys_and_values/ppermute | solution.py:439
  11.7 0.8 dynamic-slice_bitcast_fusion
  12.7 1.0 copy-done.2
  13.7 0.7 copy-done.3
  14.4 1.2 prepare.1
  15.6 0.7 collective-permute-done.rest_2_
  16.3 0.5 collective-permute-start.4
  16.8 0.5 collective-permute-start.6
  18.4 12.7 %attend.1 = (bf16[64,2944]{1,0:T(8,128)(2,1)S(1)}, bf16[64,2944]{1,0:T(8,128)(2,1)S(1)}) custom-call(s32[2]{0:T(128)S(1)} %pad_add_fusion.place, f32[32]{0:T(128)S(1)} %copy-done.4, bf16[4096,64]{1,0:T(8,128)(2,1)S(1)} %get-tuple-element.71.q_ref, f32[128,1024]{1,0:T(8,128)S(1)} %get-tuple-element.72.bias, bf16[2880,2048]{1,0:T(8,128)(2,1)} %bitcast.13, ...), custom_call_target="tpu_custom_call" | custom-call | flops 2583691264 | bytes 11796480 | tf_op jit(solution)/shard_map/attention/attend/pallas_call | solution.py:201
  31.2 1.6 %collective-permute-start.7 = (bf16[64,2944]{1,0:T(8,128)(2,1)S(1)}, bf16[64,2944]{1,0:T(8,128)(2,1)S(1)}, u32[]{:S(2)}, u32[]{:S(2)}) collective-permute-start(bf16[64,2944]{1,0:T(8,128)(2,1)S(1)} %get-tuple-element.80), channel_id=1, source_target_pairs={{0,1},{1,0},{2,3},{3,2},{4,5},{5,4},{6,7},{7,6},{8,9},{9,8},{10,11... | collective-permute-start | bytes 1130504 | tf_op jit(solution)/shard_map/norm/ppermute | solution.py:413
  33.3 8.3 %load.1 = (bf16[1440,2880]{1,0:T(8,128)(2,1)S(1)}, bf16[2,1440,2880]{2,1,0:T(8,128)(2,1)S(1)}, f32[8,128]{1,0:T(8,128)S(1)}) custom-call(bf16[1440,2880]{1,0:T(8,128)(2,1)} %bitcast.14, bf16[2,1440,2880]{2,1,0:T(8,128)(2,1)} %bitcast.12, bf16[64,2944]{1,0:T(8,128)(2,1)S(1)} %get-tuple-element.82.refs_2_.refs_0_), custom_call_target="tpu_custom_call" | custom-call | bytes 49766400 | tf_op jit(solution)/shard_map/norm/load/pallas_call | solution.py:40
  41.7 0.6 collective-permute-done.7.refs_1_
  42.2 0.8 norm_and_gates.1
  43.0 4.5 %collective-permute-start.9 = (bf16[64,2944]{1,0:T(8,128)(2,1)S(1)}, bf16[64,2944]{1,0:T(8,128)(2,1)S(1)}, u32[]{:S(2)}, u32[]{:S(2)}) collective-permute-start(bf16[64,2944]{1,0:T(8,128)(2,1)S(1)} %get-tuple-element.87.refs_0_), channel_id=1, source_target_pairs={{0,4},{2,6},{4,12},{6,14},{8,0},{10,2},{12,8},{14,10},{1,5},{3,7},... | collective-permute-start | bytes 1130504 | tf_op jit(solution)/shard_map/rows_of_chips/ppermute | solution.py:410
  47.4 1.5 %collective-permute-start.8 = (bf16[64,2944]{1,0:T(8,128)(2,1)S(1)}, bf16[64,2944]{1,0:T(8,128)(2,1)S(1)}, u32[]{:S(2)}, u32[]{:S(2)}) collective-permute-start(bf16[64,2944]{1,0:T(8,128)(2,1)S(1)} %get-tuple-element.87.refs_0_), channel_id=1, source_target_pairs={{0,1},{1,0},{2,3},{3,2},{4,5},{5,4},{6,7},{7,6},{8,9},{9,8},{10,11... | collective-permute-start | bytes 1130504 | tf_op jit(solution)/shard_map/rows_of_chips/ppermute | solution.py:413
  48.9 8.9 %collective-permute-done.9.refs_0_ = bf16[64,2944]{1,0:T(8,128)(2,1)S(1)} collective-permute-done((bf16[64,2944]{1,0:T(8,128)(2,1)S(1)}, bf16[64,2944]{1,0:T(8,128)(2,1)S(1)}, u32[]{:S(2)}, u32[]{:S(2)}) %collective-permute-start.9) | collective-permute-done | bytes 376864 | tf_op jit(solution)/shard_map/rows_of_chips/ppermute | solution.py:410
  57.8 0.5 collective-permute-start.11
  58.5 1.5 %collective-permute-start.12 = (bf16[64,2944]{1,0:T(8,128)(2,1)S(1)}, bf16[64,2944]{1,0:T(8,128)(2,1)S(1)}, u32[]{:S(2)}, u32[]{:S(2)}) collective-permute-start(bf16[64,2944]{1,0:T(8,128)(2,1)S(1)} %collective-permute-done.9.refs_0_), channel_id=1, source_target_pairs={{0,1},{1,0},{2,3},{3,2},{4,5},{5,4},{6,7},{7,6},{8,9},{9,8},{10,11... | collective-permute-start | bytes 1130504 | tf_op jit(solution)/shard_map/rows_of_chips/ppermute | solution.py:413
  60.0 8.6 %expert_rows.4 = (bf16[64,2944]{1,0:T(8,128)(2,1)S(1)}, bf16[64,2944]{1,0:T(8,128)(2,1)S(1)}, bf16[128,2944]{1,0:T(8,128)(2,1)S(1)}, f32[8,128]{1,0:T(8,128)S(1)}) custom-call(s32[2]{0:T(128)S(1)} %pad_add_fusion.place, bf16[2,1440,2880]{2,1,0:T(8,128)(2,1)S(1)} %get-tuple-element.78.gate_up, bf16[1440,2880]{1,0:T(8,128)(2,1)S(1)} %get-tuple-element.79.down, ...), custom_call_target="tpu_custom_call" | custom-call | flops 6370099200 | bytes 24883200 | tf_op jit(solution)/shard_map/experts/expert_rows/pallas_call | solution.py:323
  68.6 1.3 collective-permute-done.13.refs_0_
  69.9 0.5 collective-permute-start.15
  70.4 2.3 %collective-permute-start.17 = (bf16[64,2944]{1,0:T(8,128)(2,1)S(1)}, bf16[64,2944]{1,0:T(8,128)(2,1)S(1)}, u32[]{:S(2)}, u32[]{:S(2)}) collective-permute-start(bf16[64,2944]{1,0:T(8,128)(2,1)S(1)} %collective-permute-done.13.refs_0_), channel_id=1, source_target_pairs={{0,4},{2,6},{4,12},{6,14},{8,0},{10,2},{12,8},{14,10},{1,5},{3,7},... | collective-permute-start | bytes 1130504 | tf_op jit(solution)/shard_map/rows_of_chips/ppermute | solution.py:410
  72.7 1.5 %collective-permute-start.16 = (bf16[64,2944]{1,0:T(8,128)(2,1)S(1)}, bf16[64,2944]{1,0:T(8,128)(2,1)S(1)}, u32[]{:S(2)}, u32[]{:S(2)}) collective-permute-start(bf16[64,2944]{1,0:T(8,128)(2,1)S(1)} %collective-permute-done.13.refs_0_), channel_id=1, source_target_pairs={{0,1},{1,0},{2,3},{3,2},{4,5},{5,4},{6,7},{7,6},{8,9},{9,8},{10,11... | collective-permute-start | bytes 1130504 | tf_op jit(solution)/shard_map/rows_of_chips/ppermute | solution.py:413
  74.2 8.6 %expert_rows.5 = (bf16[64,2944]{1,0:T(8,128)(2,1)S(1)}, bf16[64,2944]{1,0:T(8,128)(2,1)S(1)}, bf16[128,2944]{1,0:T(8,128)(2,1)S(1)}, f32[8,128]{1,0:T(8,128)S(1)}) custom-call(s32[2]{0:T(128)S(1)} %pad_add_fusion.place, bf16[2,1440,2880]{2,1,0:T(8,128)(2,1)S(1)} %get-tuple-element.78.gate_up, bf16[1440,2880]{1,0:T(8,128)(2,1)S(1)} %get-tuple-element.79.down, ...), custom_call_target="tpu_custom_call" | custom-call | flops 6370099200 | bytes 24883200 | tf_op jit(solution)/shard_map/experts/expert_rows/pallas_call | solution.py:323
  83.1 1.3 collective-permute-start.21
  85.4 1.6 %collective-permute-start.22 = (bf16[64,2944]{1,0:T(8,128)(2,1)S(1)}, bf16[64,2944]{1,0:T(8,128)(2,1)S(1)}, u32[]{:S(2)}, u32[]{:S(2)}) collective-permute-start(bf16[64,2944]{1,0:T(8,128)(2,1)S(1)} %add_convert_fusion.3), channel_id=1, source_target_pairs={{0,1},{1,0},{2,3},{3,2},{4,5},{5,4},{6,7},{7,6},{8,9},{9,8},{10,11... | collective-permute-start | bytes 1130504 | tf_op jit(solution)/shard_map/sum_back/ppermute | solution.py:413
  87.0 8.6 %expert_rows.6 = (bf16[64,2944]{1,0:T(8,128)(2,1)S(1)}, bf16[64,2944]{1,0:T(8,128)(2,1)S(1)}, bf16[128,2944]{1,0:T(8,128)(2,1)S(1)}, f32[8,128]{1,0:T(8,128)S(1)}) custom-call(s32[2]{0:T(128)S(1)} %pad_add_fusion.place, bf16[2,1440,2880]{2,1,0:T(8,128)(2,1)S(1)} %get-tuple-element.78.gate_up, bf16[1440,2880]{1,0:T(8,128)(2,1)S(1)} %get-tuple-element.79.down, ...), custom_call_target="tpu_custom_call" | custom-call | flops 6370099200 | bytes 24883200 | tf_op jit(solution)/shard_map/experts/expert_rows/pallas_call | solution.py:323
  95.6 0.6 collective-permute-done.22
  96.3 0.5 collective-permute-start.30
  97.0 1.2 collective-permute-start.27
  98.2 0.5 collective-permute-start.25
  98.8 1.6 %collective-permute-start.26 = (bf16[64,2944]{1,0:T(8,128)(2,1)S(1)}, bf16[64,2944]{1,0:T(8,128)(2,1)S(1)}, u32[]{:S(2)}, u32[]{:S(2)}) collective-permute-start(bf16[64,2944]{1,0:T(8,128)(2,1)S(1)} %add_convert_fusion.2), channel_id=1, source_target_pairs={{0,1},{1,0},{2,3},{3,2},{4,5},{5,4},{6,7},{7,6},{8,9},{9,8},{10,11... | collective-permute-start | bytes 1130504 | tf_op jit(solution)/shard_map/sum_back/ppermute | solution.py:413
  100.7 8.6 %expert_rows.7 = (bf16[64,2944]{1,0:T(8,128)(2,1)S(1)}, bf16[64,2944]{1,0:T(8,128)(2,1)S(1)}, bf16[128,2944]{1,0:T(8,128)(2,1)S(1)}, f32[8,128]{1,0:T(8,128)S(1)}) custom-call(s32[2]{0:T(128)S(1)} %pad_add_fusion.place, bf16[2,1440,2880]{2,1,0:T(8,128)(2,1)S(1)} %get-tuple-element.78.gate_up, bf16[1440,2880]{1,0:T(8,128)(2,1)S(1)} %get-tuple-element.79.down, ...), custom_call_target="tpu_custom_call" | custom-call | flops 6370099200 | bytes 24883200 | tf_op jit(solution)/shard_map/experts/expert_rows/pallas_call | solution.py:323
  109.7 1.2 collective-permute-start.32
  111.0 1.2 collective-permute-start.35
  112.3 1.6 %collective-permute-start.29 = (bf16[64,1024]{1,0:T(8,128)(2,1)S(1)}, bf16[64,1024]{1,0:T(8,128)(2,1)S(1)}, u32[]{:S(2)}, u32[]{:S(2)}) collective-permute-start(bf16[64,1024]{1,0:T(8,128)(2,1)S(1)} %add_convert_fusion.9), channel_id=1, source_target_pairs={{0,1},{1,0},{2,3},{3,2},{4,5},{5,4},{6,7},{7,6},{8,9},{9,8},{10,11... | collective-permute-start | bytes 393224 | tf_op jit(solution)/shard_map/sum_back/ppermute | solution.py:413
  113.9 0.6 collective-permute-start.34
  114.5 4.2 %collective-permute-done.29 = bf16[64,1024]{1,0:T(8,128)(2,1)S(1)} collective-permute-done((bf16[64,1024]{1,0:T(8,128)(2,1)S(1)}, bf16[64,1024]{1,0:T(8,128)(2,1)S(1)}, u32[]{:S(2)}, u32[]{:S(2)}) %collective-permute-start.29) | collective-permute-done | bytes 131104 | tf_op jit(solution)/shard_map/sum_back/ppermute | solution.py:413
  118.8 1.6 %collective-permute-start.31 = (bf16[64,2944]{1,0:T(8,128)(2,1)S(1)}, bf16[64,2944]{1,0:T(8,128)(2,1)S(1)}, u32[]{:S(2)}, u32[]{:S(2)}) collective-permute-start(bf16[64,2944]{1,0:T(8,128)(2,1)S(1)} %add_convert_fusion), channel_id=1, source_target_pairs={{0,1},{1,0},{2,3},{3,2},{4,5},{5,4},{6,7},{7,6},{8,9},{9,8},{10,11... | collective-permute-start | bytes 1130504 | tf_op jit(solution)/shard_map/sum_back/ppermute | solution.py:413
  120.4 1.4 %collective-permute-done.35 = bf16[64,1920]{1,0:T(8,128)(2,1)S(1)} collective-permute-done((bf16[64,1920]{1,0:T(8,128)(2,1)S(1)}, bf16[64,1920]{1,0:T(8,128)(2,1)S(1)}, u32[]{:S(2)}, u32[]{:S(2)}) %collective-permute-start.35) | collective-permute-done | bytes 245792 | tf_op jit(solution)/shard_map/sum_back/ppermute | solution.py:410
  121.8 2.2 %collective-permute-done.34 = bf16[64,1920]{1,0:T(8,128)(2,1)S(1)} collective-permute-done((bf16[64,1920]{1,0:T(8,128)(2,1)S(1)}, bf16[64,1920]{1,0:T(8,128)(2,1)S(1)}, u32[]{:S(2)}, u32[]{:S(2)}) %collective-permute-start.34) | collective-permute-done | bytes 245792 | tf_op jit(solution)/shard_map/sum_back/ppermute | solution.py:413
  124.1 1.5 %collective-permute-start.36 = (bf16[64,1920]{1,0:T(8,128)(2,1)S(1)}, bf16[64,1920]{1,0:T(8,128)(2,1)S(1)}, u32[]{:S(2)}, u32[]{:S(2)}) collective-permute-start(bf16[64,1920]{1,0:T(8,128)(2,1)S(1)} %add_convert_fusion.4), channel_id=1, source_target_pairs={{0,4},{2,6},{4,12},{6,14},{8,0},{10,2},{12,8},{14,10},{1,5},{3,7},... | collective-permute-start | bytes 737288 | tf_op jit(solution)/shard_map/sum_back/ppermute | solution.py:410
  125.7 1.2 collective-permute-start.33
  126.9 6.9 %collective-permute-done.33.refs_4_ = bf16[64,1024]{1,0:T(8,128)(2,1)S(1)} collective-permute-done((bf16[64,1024]{1,0:T(8,128)(2,1)S(1)}, bf16[64,1024]{1,0:T(8,128)(2,1)S(1)}, u32[]{:S(2)}, u32[]{:S(2)}) %collective-permute-start.33) | collective-permute-done | bytes 131104 | tf_op jit(solution)/shard_map/sum_back/ppermute | solution.py:410
  133.8 1.0 finish.1
  (75 shorter events, 4.9 us)
Async XLA Ops:
  0.0 17.4 %copy-start = (bf16[128,2880]{0,1:T(8,128)(2,1)S(1)}, bf16[128,2880]{0,1:T(8,128)(2,1)}, u32[]{:S(2)}) copy-start(bf16[128,2880]{0,1:T(8,128)(2,1)} %param.17) | copy-start | bytes 2211844
  0.0 18.4 %copy-start.4 = (f32[32]{0:T(128)S(1)}, f32[32]{0:T(128)}, u32[]{:S(2)}) copy-start(f32[32]{0:T(128)} %sinks.1) | copy-start | bytes 388
  1.0 14.6 %collective-permute-start.2 = (bf16[128,512]{1,0:T(8,128)(2,1)S(1)}, bf16[128,512]{1,0:T(8,128)(2,1)S(1)}, u32[]{:S(2)}, u32[]{:S(2)}) collective-permute-start(bf16[128,512]{1,0:T(8,128)(2,1)S(1)} %side_by_side.1.rest_0_), channel_id=1, source_target_pairs={{0,12},{2,14},{1,13},{3,15},{16,28},{18,30},{17,29},{19,31}} | collective-permute-start | bytes 393224 | tf_op jit(solution)/shard_map/keys_and_values/ppermute | solution.py:439
  7.9 7.7 %collective-permute-start.1 = (bf16[128,512]{1,0:T(8,128)(2,1)S(1)}, bf16[128,512]{1,0:T(8,128)(2,1)S(1)}, u32[]{:S(2)}, u32[]{:S(2)}) collective-permute-start(bf16[128,512]{1,0:T(8,128)(2,1)S(1)} %side_by_side.1.rest_0_), channel_id=1, source_target_pairs={{0,8},{2,10},{4,12},{6,14},{1,9},{3,11},{5,13},{7,15},{16,24},{18,... | collective-permute-start | bytes 393224 | tf_op jit(solution)/shard_map/keys_and_values/ppermute | solution.py:439
  9.2 7.1 %collective-permute-start = (bf16[128,512]{1,0:T(8,128)(2,1)S(1)}, bf16[128,512]{1,0:T(8,128)(2,1)S(1)}, u32[]{:S(2)}, u32[]{:S(2)}) collective-permute-start(bf16[128,512]{1,0:T(8,128)(2,1)S(1)} %side_by_side.1.rest_0_), channel_id=1, source_target_pairs={{0,4},{2,6},{4,8},{6,10},{8,12},{10,14},{1,5},{3,7},{5,9},{7,11},{... | collective-permute-start | bytes 393224 | tf_op jit(solution)/shard_map/keys_and_values/ppermute | solution.py:439
  12.7 1.0 copy-start.2
  13.7 0.7 copy-start.3
  16.3 1.3 %collective-permute-start.3 = (bf16[128,512]{1,0:T(8,128)(2,1)S(1)}, bf16[128,512]{1,0:T(8,128)(2,1)S(1)}, u32[]{:S(2)}, u32[]{:S(2)}) collective-permute-start(bf16[128,512]{1,0:T(8,128)(2,1)S(1)} %side_by_side.1.rest_0_), channel_id=1, source_target_pairs={{0,2},{2,0},{4,6},{6,4},{8,10},{10,8},{12,14},{14,12},{1,3},{3,1},... | collective-permute-start | bytes 393224 | tf_op jit(solution)/shard_map/attention/ppermute | solution.py:407
  16.3 1.5 %collective-permute-start.4 = (bf16[128,512]{1,0:T(8,128)(2,1)S(1)}, bf16[128,512]{1,0:T(8,128)(2,1)S(1)}, u32[]{:S(2)}, u32[]{:S(2)}) collective-permute-start(bf16[128,512]{1,0:T(8,128)(2,1)S(1)} %collective-permute-done.rest_2_), channel_id=1, source_target_pairs={{0,2},{2,0},{4,6},{6,4},{8,10},{10,8},{12,14},{14,12},{1,3},{3,1},... | collective-permute-start | bytes 393224 | tf_op jit(solution)/shard_map/attention/ppermute | solution.py:407
  16.8 1.3 %collective-permute-start.5 = (bf16[128,512]{1,0:T(8,128)(2,1)S(1)}, bf16[128,512]{1,0:T(8,128)(2,1)S(1)}, u32[]{:S(2)}, u32[]{:S(2)}) collective-permute-start(bf16[128,512]{1,0:T(8,128)(2,1)S(1)} %collective-permute-done.1.rest_4_), channel_id=1, source_target_pairs={{0,2},{2,0},{4,6},{6,4},{8,10},{10,8},{12,14},{14,12},{1,3},{3,1},... | collective-permute-start | bytes 393224 | tf_op jit(solution)/shard_map/attention/ppermute | solution.py:407
  16.8 1.5 %collective-permute-start.6 = (bf16[128,512]{1,0:T(8,128)(2,1)S(1)}, bf16[128,512]{1,0:T(8,128)(2,1)S(1)}, u32[]{:S(2)}, u32[]{:S(2)}) collective-permute-start(bf16[128,512]{1,0:T(8,128)(2,1)S(1)} %collective-permute-done.2.rest_6_), channel_id=1, source_target_pairs={{0,2},{2,0},{4,6},{6,4},{8,10},{10,8},{12,14},{14,12},{1,3},{3,1},... | collective-permute-start | bytes 393224 | tf_op jit(solution)/shard_map/attention/ppermute | solution.py:407
  18.4 14.3 %copy-start.7 = (s32[128,4]{0,1:T(4,128)S(1)}, s32[128,4]{0,1:T(4,128)}, u32[]{:S(2)}) copy-start(s32[128,4]{0,1:T(4,128)} %param.18) | copy-start | bytes 6148
  18.4 14.4 %copy-start.6 = (f32[2880]{0:T(1024)S(1)}, f32[2880]{0:T(1024)}, u32[]{:S(2)}) copy-start(f32[2880]{0:T(1024)} %param.20) | copy-start | bytes 34564
  31.1 2.1 %copy-start.5 = (bf16[2880,8]{0,1:T(8,128)(2,1)S(1)}, bf16[2880,8]{0,1:T(8,128)(2,1)}, u32[]{:S(2)}) copy-start(bf16[2880,8]{0,1:T(8,128)(2,1)} %param.21) | copy-start | bytes 138244
  31.2 11.1 %collective-permute-start.7 = (bf16[64,2944]{1,0:T(8,128)(2,1)S(1)}, bf16[64,2944]{1,0:T(8,128)(2,1)S(1)}, u32[]{:S(2)}, u32[]{:S(2)}) collective-permute-start(bf16[64,2944]{1,0:T(8,128)(2,1)S(1)} %get-tuple-element.80), channel_id=1, source_target_pairs={{0,1},{1,0},{2,3},{3,2},{4,5},{5,4},{6,7},{7,6},{8,9},{9,8},{10,11... | collective-permute-start | bytes 1130504 | tf_op jit(solution)/shard_map/norm/ppermute | solution.py:413
  43.0 14.8 %collective-permute-start.9 = (bf16[64,2944]{1,0:T(8,128)(2,1)S(1)}, bf16[64,2944]{1,0:T(8,128)(2,1)S(1)}, u32[]{:S(2)}, u32[]{:S(2)}) collective-permute-start(bf16[64,2944]{1,0:T(8,128)(2,1)S(1)} %get-tuple-element.87.refs_0_), channel_id=1, source_target_pairs={{0,4},{2,6},{4,12},{6,14},{8,0},{10,2},{12,8},{14,10},{1,5},{3,7},... | collective-permute-start | bytes 1130504 | tf_op jit(solution)/shard_map/rows_of_chips/ppermute | solution.py:410
  47.4 10.4 %collective-permute-start.8 = (bf16[64,2944]{1,0:T(8,128)(2,1)S(1)}, bf16[64,2944]{1,0:T(8,128)(2,1)S(1)}, u32[]{:S(2)}, u32[]{:S(2)}) collective-permute-start(bf16[64,2944]{1,0:T(8,128)(2,1)S(1)} %get-tuple-element.87.refs_0_), channel_id=1, source_target_pairs={{0,1},{1,0},{2,3},{3,2},{4,5},{5,4},{6,7},{7,6},{8,9},{9,8},{10,11... | collective-permute-start | bytes 1130504 | tf_op jit(solution)/shard_map/rows_of_chips/ppermute | solution.py:413
  57.8 2.2 %collective-permute-start.10 = (bf16[64,2944]{1,0:T(8,128)(2,1)S(1)}, bf16[64,2944]{1,0:T(8,128)(2,1)S(1)}, u32[]{:S(2)}, u32[]{:S(2)}) collective-permute-start(bf16[64,2944]{1,0:T(8,128)(2,1)S(1)} %get-tuple-element.87.refs_0_), channel_id=1, source_target_pairs={{0,2},{2,0},{4,6},{6,4},{8,10},{10,8},{12,14},{14,12},{1,3},{3,1},... | collective-permute-start | bytes 1130504 | tf_op jit(solution)/shard_map/experts/ppermute | solution.py:407
  57.8 2.2 %collective-permute-start.11 = (bf16[64,2944]{1,0:T(8,128)(2,1)S(1)}, bf16[64,2944]{1,0:T(8,128)(2,1)S(1)}, u32[]{:S(2)}, u32[]{:S(2)}) collective-permute-start(bf16[64,2944]{1,0:T(8,128)(2,1)S(1)} %collective-permute-done.8.refs_1_), channel_id=1, source_target_pairs={{0,2},{2,0},{4,6},{6,4},{8,10},{10,8},{12,14},{14,12},{1,3},{3,1},... | collective-permute-start | bytes 1130504 | tf_op jit(solution)/shard_map/experts/ppermute | solution.py:407
  58.3 11.6 %collective-permute-start.13 = (bf16[64,2944]{1,0:T(8,128)(2,1)S(1)}, bf16[64,2944]{1,0:T(8,128)(2,1)S(1)}, u32[]{:S(2)}, u32[]{:S(2)}) collective-permute-start(bf16[64,2944]{1,0:T(8,128)(2,1)S(1)} %collective-permute-done.9.refs_0_), channel_id=1, source_target_pairs={{0,4},{2,6},{4,12},{6,14},{8,0},{10,2},{12,8},{14,10},{1,5},{3,7},... | collective-permute-start | bytes 1130504 | tf_op jit(solution)/shard_map/rows_of_chips/ppermute | solution.py:410
  58.5 11.4 %collective-permute-start.12 = (bf16[64,2944]{1,0:T(8,128)(2,1)S(1)}, bf16[64,2944]{1,0:T(8,128)(2,1)S(1)}, u32[]{:S(2)}, u32[]{:S(2)}) collective-permute-start(bf16[64,2944]{1,0:T(8,128)(2,1)S(1)} %collective-permute-done.9.refs_0_), channel_id=1, source_target_pairs={{0,1},{1,0},{2,3},{3,2},{4,5},{5,4},{6,7},{7,6},{8,9},{9,8},{10,11... | collective-permute-start | bytes 1130504 | tf_op jit(solution)/shard_map/rows_of_chips/ppermute | solution.py:413
  69.9 4.3 %collective-permute-start.14 = (bf16[64,2944]{1,0:T(8,128)(2,1)S(1)}, bf16[64,2944]{1,0:T(8,128)(2,1)S(1)}, u32[]{:S(2)}, u32[]{:S(2)}) collective-permute-start(bf16[64,2944]{1,0:T(8,128)(2,1)S(1)} %collective-permute-done.9.refs_0_), channel_id=1, source_target_pairs={{0,2},{2,0},{4,6},{6,4},{8,10},{10,8},{12,14},{14,12},{1,3},{3,1},... | collective-permute-start | bytes 1130504 | tf_op jit(solution)/shard_map/experts/ppermute | solution.py:407
  69.9 4.3 %collective-permute-start.15 = (bf16[64,2944]{1,0:T(8,128)(2,1)S(1)}, bf16[64,2944]{1,0:T(8,128)(2,1)S(1)}, u32[]{:S(2)}, u32[]{:S(2)}) collective-permute-start(bf16[64,2944]{1,0:T(8,128)(2,1)S(1)} %collective-permute-done.12.refs_1_), channel_id=1, source_target_pairs={{0,2},{2,0},{4,6},{6,4},{8,10},{10,8},{12,14},{14,12},{1,3},{3,1},... | collective-permute-start | bytes 1130504 | tf_op jit(solution)/shard_map/experts/ppermute | solution.py:407
  70.4 12.4 %collective-permute-start.17 = (bf16[64,2944]{1,0:T(8,128)(2,1)S(1)}, bf16[64,2944]{1,0:T(8,128)(2,1)S(1)}, u32[]{:S(2)}, u32[]{:S(2)}) collective-permute-start(bf16[64,2944]{1,0:T(8,128)(2,1)S(1)} %collective-permute-done.13.refs_0_), channel_id=1, source_target_pairs={{0,4},{2,6},{4,12},{6,14},{8,0},{10,2},{12,8},{14,10},{1,5},{3,7},... | collective-permute-start | bytes 1130504 | tf_op jit(solution)/shard_map/rows_of_chips/ppermute | solution.py:410
  72.7 10.4 %collective-permute-start.16 = (bf16[64,2944]{1,0:T(8,128)(2,1)S(1)}, bf16[64,2944]{1,0:T(8,128)(2,1)S(1)}, u32[]{:S(2)}, u32[]{:S(2)}) collective-permute-start(bf16[64,2944]{1,0:T(8,128)(2,1)S(1)} %collective-permute-done.13.refs_0_), channel_id=1, source_target_pairs={{0,1},{1,0},{2,3},{3,2},{4,5},{5,4},{6,7},{7,6},{8,9},{9,8},{10,11... | collective-permute-start | bytes 1130504 | tf_op jit(solution)/shard_map/rows_of_chips/ppermute | solution.py:413
  83.1 2.2 %collective-permute-start.18 = (bf16[128,2944]{1,0:T(8,128)(2,1)S(1)}, bf16[128,2944]{1,0:T(8,128)(2,1)S(1)}, u32[]{:S(2)}, u32[]{:S(2)}) collective-permute-start(bf16[128,2944]{1,0:T(8,128)(2,1)S(1)} %get-tuple-element.97), channel_id=1, source_target_pairs={{0,2},{2,0},{4,6},{6,4},{8,10},{10,8},{12,14},{14,12},{1,3},{3,1},... | collective-permute-start | bytes 2261000 | tf_op jit(solution)/shard_map/sum_back/ppermute | solution.py:407
  83.1 12.5 %collective-permute-start.21 = (bf16[64,2944]{1,0:T(8,128)(2,1)S(1)}, bf16[64,2944]{1,0:T(8,128)(2,1)S(1)}, u32[]{:S(2)}, u32[]{:S(2)}) collective-permute-start(bf16[64,2944]{1,0:T(8,128)(2,1)S(1)} %collective-permute-done.16.refs_1_), channel_id=1, source_target_pairs={{0,4},{2,6},{4,12},{6,14},{8,0},{10,2},{12,8},{14,10},{1,5},{3,7},... | collective-permute-start | bytes 1130504 | tf_op jit(solution)/shard_map/rows_of_chips/ppermute | solution.py:410
  84.4 2.7 %collective-permute-start.20 = (bf16[64,2944]{1,0:T(8,128)(2,1)S(1)}, bf16[64,2944]{1,0:T(8,128)(2,1)S(1)}, u32[]{:S(2)}, u32[]{:S(2)}) collective-permute-start(bf16[64,2944]{1,0:T(8,128)(2,1)S(1)} %collective-permute-done.16.refs_1_), channel_id=1, source_target_pairs={{0,2},{2,0},{4,6},{6,4},{8,10},{10,8},{12,14},{14,12},{1,3},{3,1},... | collective-permute-start | bytes 1130504 | tf_op jit(solution)/shard_map/experts/ppermute | solution.py:407
  84.5 2.5 %collective-permute-start.19 = (bf16[64,2944]{1,0:T(8,128)(2,1)S(1)}, bf16[64,2944]{1,0:T(8,128)(2,1)S(1)}, u32[]{:S(2)}, u32[]{:S(2)}) collective-permute-start(bf16[64,2944]{1,0:T(8,128)(2,1)S(1)} %collective-permute-done.13.refs_0_), channel_id=1, source_target_pairs={{0,2},{2,0},{4,6},{6,4},{8,10},{10,8},{12,14},{14,12},{1,3},{3,1},... | collective-permute-start | bytes 1130504 | tf_op jit(solution)/shard_map/experts/ppermute | solution.py:407
  85.4 10.9 %collective-permute-start.22 = (bf16[64,2944]{1,0:T(8,128)(2,1)S(1)}, bf16[64,2944]{1,0:T(8,128)(2,1)S(1)}, u32[]{:S(2)}, u32[]{:S(2)}) collective-permute-start(bf16[64,2944]{1,0:T(8,128)(2,1)S(1)} %add_convert_fusion.3), channel_id=1, source_target_pairs={{0,1},{1,0},{2,3},{3,2},{4,5},{5,4},{6,7},{7,6},{8,9},{9,8},{10,11... | collective-permute-start | bytes 1130504 | tf_op jit(solution)/shard_map/sum_back/ppermute | solution.py:413
  96.3 2.4 %collective-permute-start.23 = (bf16[128,2944]{1,0:T(8,128)(2,1)S(1)}, bf16[128,2944]{1,0:T(8,128)(2,1)S(1)}, u32[]{:S(2)}, u32[]{:S(2)}) collective-permute-start(bf16[128,2944]{1,0:T(8,128)(2,1)S(1)} %get-tuple-element.107), channel_id=1, source_target_pairs={{0,2},{2,0},{4,6},{6,4},{8,10},{10,8},{12,14},{14,12},{1,3},{3,1},... | collective-permute-start | bytes 2261000 | tf_op jit(solution)/shard_map/sum_back/ppermute | solution.py:407
  96.3 13.2 %collective-permute-start.30 = (bf16[128,2944]{1,0:T(8,128)(2,1)S(1)}, bf16[128,2944]{1,0:T(8,128)(2,1)S(1)}, u32[]{:S(2)}, u32[]{:S(2)}) collective-permute-start(bf16[128,2944]{1,0:T(8,128)(2,1)S(1)} %get-tuple-element.122), channel_id=1, source_target_pairs={{0,2},{2,0},{4,6},{6,4},{8,10},{10,8},{12,14},{14,12},{1,3},{3,1},... | collective-permute-start | bytes 2261000 | tf_op jit(solution)/shard_map/sum_back/ppermute | solution.py:407
  97.0 12.3 %collective-permute-start.27 = (bf16[64,2944]{1,0:T(8,128)(2,1)S(1)}, bf16[64,2944]{1,0:T(8,128)(2,1)S(1)}, u32[]{:S(2)}, u32[]{:S(2)}) collective-permute-start(bf16[64,2944]{1,0:T(8,128)(2,1)S(1)} %add_convert_fusion.1), channel_id=1, source_target_pairs={{0,4},{2,6},{4,12},{6,14},{8,0},{10,2},{12,8},{14,10},{1,5},{3,7},... | collective-permute-start | bytes 1130504 | tf_op jit(solution)/shard_map/sum_back/ppermute | solution.py:410
  98.2 2.2 %collective-permute-start.24 = (bf16[64,2944]{1,0:T(8,128)(2,1)S(1)}, bf16[64,2944]{1,0:T(8,128)(2,1)S(1)}, u32[]{:S(2)}, u32[]{:S(2)}) collective-permute-start(bf16[64,2944]{1,0:T(8,128)(2,1)S(1)} %collective-permute-done.17.refs_0_), channel_id=1, source_target_pairs={{0,2},{2,0},{4,6},{6,4},{8,10},{10,8},{12,14},{14,12},{1,3},{3,1},... | collective-permute-start | bytes 1130504 | tf_op jit(solution)/shard_map/experts/ppermute | solution.py:407
  98.2 2.5 %collective-permute-start.25 = (bf16[64,2944]{1,0:T(8,128)(2,1)S(1)}, bf16[64,2944]{1,0:T(8,128)(2,1)S(1)}, u32[]{:S(2)}, u32[]{:S(2)}) collective-permute-start(bf16[64,2944]{1,0:T(8,128)(2,1)S(1)} %collective-permute-done.21.refs_1_), channel_id=1, source_target_pairs={{0,2},{2,0},{4,6},{6,4},{8,10},{10,8},{12,14},{14,12},{1,3},{3,1},... | collective-permute-start | bytes 1130504 | tf_op jit(solution)/shard_map/experts/ppermute | solution.py:407
  98.8 10.7 %collective-permute-start.26 = (bf16[64,2944]{1,0:T(8,128)(2,1)S(1)}, bf16[64,2944]{1,0:T(8,128)(2,1)S(1)}, u32[]{:S(2)}, u32[]{:S(2)}) collective-permute-start(bf16[64,2944]{1,0:T(8,128)(2,1)S(1)} %add_convert_fusion.2), channel_id=1, source_target_pairs={{0,1},{1,0},{2,3},{3,2},{4,5},{5,4},{6,7},{7,6},{8,9},{9,8},{10,11... | collective-permute-start | bytes 1130504 | tf_op jit(solution)/shard_map/sum_back/ppermute | solution.py:413
  109.5 2.7 %collective-permute-start.28 = (bf16[128,2944]{1,0:T(8,128)(2,1)S(1)}, bf16[128,2944]{1,0:T(8,128)(2,1)S(1)}, u32[]{:S(2)}, u32[]{:S(2)}) collective-permute-start(bf16[128,2944]{1,0:T(8,128)(2,1)S(1)} %get-tuple-element.120), channel_id=1, source_target_pairs={{0,2},{2,0},{4,6},{6,4},{8,10},{10,8},{12,14},{14,12},{1,3},{3,1},... | collective-permute-start | bytes 2261000 | tf_op jit(solution)/shard_map/sum_back/ppermute | solution.py:407
  109.7 15.9 %collective-permute-start.32 = (bf16[64,1024]{1,0:T(8,128)(2,1)S(1)}, bf16[64,1024]{1,0:T(8,128)(2,1)S(1)}, u32[]{:S(2)}, u32[]{:S(2)}) collective-permute-start(bf16[64,1024]{1,0:T(8,128)(2,1)S(1)} %add_convert_fusion.8), channel_id=1, source_target_pairs={{0,4},{2,6},{4,12},{6,14},{8,0},{10,2},{12,8},{14,10},{1,5},{3,7},... | collective-permute-start | bytes 393224 | tf_op jit(solution)/shard_map/sum_back/ppermute | solution.py:410
  111.0 10.8 %collective-permute-start.35 = (bf16[64,1920]{1,0:T(8,128)(2,1)S(1)}, bf16[64,1920]{1,0:T(8,128)(2,1)S(1)}, u32[]{:S(2)}, u32[]{:S(2)}) collective-permute-start(bf16[64,1920]{1,0:T(8,128)(2,1)S(1)} %add_convert_fusion.5), channel_id=1, source_target_pairs={{0,4},{2,6},{4,12},{6,14},{8,0},{10,2},{12,8},{14,10},{1,5},{3,7},... | collective-permute-start | bytes 737288 | tf_op jit(solution)/shard_map/sum_back/ppermute | solution.py:410
  112.3 6.4 %collective-permute-start.29 = (bf16[64,1024]{1,0:T(8,128)(2,1)S(1)}, bf16[64,1024]{1,0:T(8,128)(2,1)S(1)}, u32[]{:S(2)}, u32[]{:S(2)}) collective-permute-start(bf16[64,1024]{1,0:T(8,128)(2,1)S(1)} %add_convert_fusion.9), channel_id=1, source_target_pairs={{0,1},{1,0},{2,3},{3,2},{4,5},{5,4},{6,7},{7,6},{8,9},{9,8},{10,11... | collective-permute-start | bytes 393224 | tf_op jit(solution)/shard_map/sum_back/ppermute | solution.py:413
  113.9 10.1 %collective-permute-start.34 = (bf16[64,1920]{1,0:T(8,128)(2,1)S(1)}, bf16[64,1920]{1,0:T(8,128)(2,1)S(1)}, u32[]{:S(2)}, u32[]{:S(2)}) collective-permute-start(bf16[64,1920]{1,0:T(8,128)(2,1)S(1)} %add_convert_fusion.6), channel_id=1, source_target_pairs={{0,1},{1,0},{2,3},{3,2},{4,5},{5,4},{6,7},{7,6},{8,9},{9,8},{10,11... | collective-permute-start | bytes 737288 | tf_op jit(solution)/shard_map/sum_back/ppermute | solution.py:413
  118.8 15.0 %collective-permute-start.31 = (bf16[64,2944]{1,0:T(8,128)(2,1)S(1)}, bf16[64,2944]{1,0:T(8,128)(2,1)S(1)}, u32[]{:S(2)}, u32[]{:S(2)}) collective-permute-start(bf16[64,2944]{1,0:T(8,128)(2,1)S(1)} %add_convert_fusion), channel_id=1, source_target_pairs={{0,1},{1,0},{2,3},{3,2},{4,5},{5,4},{6,7},{7,6},{8,9},{9,8},{10,11... | collective-permute-start | bytes 1130504 | tf_op jit(solution)/shard_map/sum_back/ppermute | solution.py:413
  124.0 10.8 %copy-start.1 = (bf16[128,2880]{0,1:T(8,128)(2,1)S(1)}, bf16[128,2880]{0,1:T(8,128)(2,1)}, u32[]{:S(2)}) copy-start(bf16[128,2880]{0,1:T(8,128)(2,1)} %param.17) | copy-start | bytes 2211844
  124.1 9.7 %collective-permute-start.36 = (bf16[64,1920]{1,0:T(8,128)(2,1)S(1)}, bf16[64,1920]{1,0:T(8,128)(2,1)S(1)}, u32[]{:S(2)}, u32[]{:S(2)}) collective-permute-start(bf16[64,1920]{1,0:T(8,128)(2,1)S(1)} %add_convert_fusion.4), channel_id=1, source_target_pairs={{0,4},{2,6},{4,12},{6,14},{8,0},{10,2},{12,8},{14,10},{1,5},{3,7},... | collective-permute-start | bytes 737288 | tf_op jit(solution)/shard_map/sum_back/ppermute | solution.py:410
  125.7 8.1 %collective-permute-start.33 = (bf16[64,1024]{1,0:T(8,128)(2,1)S(1)}, bf16[64,1024]{1,0:T(8,128)(2,1)S(1)}, u32[]{:S(2)}, u32[]{:S(2)}) collective-permute-start(bf16[64,1024]{1,0:T(8,128)(2,1)S(1)} %add_convert_fusion.7), channel_id=1, source_target_pairs={{0,4},{2,6},{4,12},{6,14},{8,0},{10,2},{12,8},{14,10},{1,5},{3,7},... | collective-permute-start | bytes 393224 | tf_op jit(solution)/shard_map/sum_back/ppermute | solution.py:410
